TPU v7x, 32 devices: a whole 2x2x4 slice. The times are simulated.
32 devices in a mesh: seq: 8 (over z, x), head: 4 (over y, core).
Axes of the slice: x: 2, y: 2, z: 4, core: 2. Of those that a mesh axis runs over, the one named last changes fastest.
Arguments:
- layer_input: bfloat16 [1024, 8192], P('seq'), may hold values from -6 to 6
- beta_weight: bfloat16 [32, 8192], P('head'), may hold values from -0.0625 to 0.0625
- decay_weight: bfloat16 [32, 8192], P('head'), may hold values from -0.0625 to 0.0625
- log_rate: float32 [32], P('head'), may hold values from -11.5 to -3
- decay_bias: float32 [32], P('head'), may hold values from -2 to 1
- delta_query: bfloat16 [1024, 4096], P('seq', 'head'), may hold values from -6 to 6
- delta_key: bfloat16 [1024, 4096], P('seq', 'head'), may hold values from -6 to 6
- delta_value: bfloat16 [1024, 4096], P('seq', 'head'), may hold values from -6 to 6
- delta_out_grad: bfloat16 [1024, 4096], P('seq', 'head'), may hold values from -6 to 6
- state_init: float32 [32, 128, 128], P('head'), may hold values from -6 to 6
- state_grad_next: float32 [32, 128, 128], P('head'), may hold values from -6 to 6
- attn_query: bfloat16 [1024, 1024], P('seq', 'head'), may hold values from -80 to 80
- attn_key: bfloat16 [1024, 1024], P('seq', 'head'), may hold values from -12 to 12
- attn_value: bfloat16 [1024, 1024], P('seq', 'head'), may hold values from -6 to 6
- attn_out_grad: bfloat16 [1024, 1024], P('seq', 'head'), may hold values from -6 to 6
Outputs:
- delta_query_grad: float32 [1024, 4096], P('seq', 'head')
- delta_key_grad: float32 [1024, 4096], P('seq', 'head')
- delta_value_grad: float32 [1024, 4096], P('seq', 'head')
- boundary_grads: float32 [8, 32, 128, 128], P('seq', 'head')
- input_grad: float32 [1024, 8192], P('seq', 'head')
- beta_weight_grad: float32 [32, 8192], P('head', 'seq')
- decay_weight_grad: float32 [32, 8192], P('head', 'seq')
- log_rate_grad: float32 [32], P('head')
- decay_bias_grad: float32 [32], P('head')
- attn_query_grad: float32 [1024, 1024], P('seq', 'head')
- attn_key_grad: float32 [1024, 1024], P('seq', 'head')
- attn_value_grad: float32 [1024, 1024], P('seq', 'head')
All inputs are finite; a program needn't handle non-finite values.
Results may differ from a plain program's by a relative error of at most 0.00035.
Values may be sent and summed in bfloat16 or wider, within the bound.
A program may use at most 128 MiB of HBM per device.

v0:
```python
import math

import jax
import jax.numpy as jnp
from jax import lax
from jax.sharding import PartitionSpec as P

STRETCH = 64
AHD = 128
WINDOW = 1024


PRECISE = lax.Precision.HIGHEST


def shifted(value, axis, by):
    length = lax.axis_size(axis)
    pairs = [(i, i + by) for i in range(length) if 0 <= i + by < length]
    return lax.ppermute(value, axis, pairs)


def dot_high(left_mat, right_mat):
    return jnp.matmul(left_mat, right_mat, precision=PRECISE)


def chain_mul(left_mat, right_mat):
    return jnp.einsum("hij,hjk->hik", left_mat, right_mat, precision=PRECISE)


def unit_rows(values):
    return values * lax.rsqrt(jnp.sum(values * values, axis=-1, keepdims=True) + 1e-06)


def stretch_step(memory, queries, key_rows, values, beta_rows, decay_log):
    span_len = queries.shape[0]
    cumulative = jnp.cumsum(decay_log)
    row_ids = lax.broadcasted_iota(jnp.int32, (span_len, span_len), 0)
    col_ids = lax.broadcasted_iota(jnp.int32, (span_len, span_len), 1)
    lower_mask = row_ids >= col_ids
    strict_mask = row_ids > col_ids
    ratios = jnp.where(
        lower_mask,
        jnp.exp(jnp.where(lower_mask, cumulative[:, None] - cumulative[None, :], 0.0)),
        0.0,
    )
    gram_keys = dot_high(key_rows, key_rows.T)
    system_mat = jnp.eye(span_len, dtype=queries.dtype) + jnp.where(
        strict_mask, beta_rows[:, None] * ratios * gram_keys, 0.0
    )
    growths = jnp.exp(cumulative)
    right_side = beta_rows[:, None] * (values - growths[:, None] * dot_high(key_rows, memory))
    updates = jax.scipy.linalg.solve_triangular(
        system_mat, right_side, lower=True, unit_diagonal=True
    )
    output = growths[:, None] * dot_high(queries, memory) + dot_high(
        ratios * dot_high(queries, key_rows.T), updates
    )
    tail_decay = jnp.exp(cumulative[-1] - cumulative)
    new_memory = jnp.exp(cumulative[-1]) * memory + dot_high(
        (key_rows * tail_decay[:, None]).T, updates
    )
    return (new_memory, output)


def block_forward(memory, q_raw, k_raw, values, beta_rows, decay_rows):
    head_count, tok_count, key_width = q_raw.shape
    span_count = tok_count // STRETCH
    queries = unit_rows(q_raw) / math.sqrt(key_width)
    key_rows = unit_rows(k_raw)

    def in_stretches(array_in):
        return jnp.swapaxes(
            array_in.reshape((head_count, span_count, STRETCH) + array_in.shape[2:]), 0, 1
        )

    pieces_all = (
        in_stretches(queries),
        in_stretches(key_rows),
        in_stretches(values),
        in_stretches(beta_rows),
        in_stretches(decay_rows),
    )
    stepper = jax.vmap(stretch_step)

    def advance(carried, pieces):
        return stepper(carried, pieces[0], pieces[1], pieces[2], pieces[3], pieces[4])

    final_mem, outputs = lax.scan(advance, memory, pieces_all)
    outputs = jnp.swapaxes(outputs, 0, 1).reshape(head_count, tok_count, values.shape[2])
    return (outputs, final_mem)


def gate_values(beta_logit, decay_input, log_rate, decay_bias):
    betas = jax.nn.sigmoid(beta_logit)
    decays = -jnp.exp(log_rate)[None, :] * jax.nn.softplus(decay_input + decay_bias[None, :])
    return (betas, decays)


def heads_first(flat_rows, head_count):
    return jnp.swapaxes(flat_rows.reshape(flat_rows.shape[0], head_count, -1), 0, 1)


def tokens_first(split_heads):
    return jnp.swapaxes(split_heads, 0, 1).reshape(split_heads.shape[1], -1)


def window_grads(q_block, k_block, v_block, grad_block, q_places, k_places):
    q_heads = q_block.reshape(q_block.shape[0], -1, AHD)
    k_heads = k_block.reshape(k_block.shape[0], -1, AHD)
    v_heads = v_block.reshape(v_block.shape[0], -1, AHD)
    g_heads = grad_block.reshape(grad_block.shape[0], -1, AHD)
    scale = 1.0 / math.sqrt(AHD)
    scores = (
        jnp.einsum("qhd,khd->hqk", q_heads, k_heads, preferred_element_type=jnp.float32) * scale
    )
    spread = q_places[:, None] - k_places[None, :]
    allowed = (spread >= 0) & (spread < WINDOW) & (k_places[None, :] >= 0)
    scores = jnp.where(allowed[None], scores, -1e30)
    weights = jax.nn.softmax(scores, axis=-1)
    g_wide = g_heads.astype(jnp.float32)
    mixed = jnp.einsum("hqk,khd->qhd", weights, v_heads.astype(jnp.float32), precision=PRECISE)
    weight_grad = jnp.einsum("qhd,khd->hqk", g_heads, v_heads, preferred_element_type=jnp.float32)
    value_grad = jnp.einsum("hqk,qhd->khd", weights, g_wide, precision=PRECISE)
    row_terms = jnp.swapaxes(jnp.sum(g_wide * mixed, axis=-1), 0, 1)
    score_grad = weights * (weight_grad - row_terms[:, :, None]) * scale
    query_grad = jnp.einsum(
        "hqk,khd->qhd", score_grad, k_heads.astype(jnp.float32), precision=PRECISE
    )
    key_grad = jnp.einsum(
        "hqk,qhd->khd", score_grad, q_heads.astype(jnp.float32), precision=PRECISE
    )
    return (
        query_grad.reshape(q_block.shape[0], -1),
        key_grad.reshape(k_block.shape[0], -1),
        value_grad.reshape(k_block.shape[0], -1),
    )


def shards(
    layer_input,
    beta_weight,
    decay_weight,
    log_rate,
    decay_bias,
    delta_query,
    delta_key,
    delta_value,
    delta_out_grad,
    state_init,
    state_grad_next,
    attn_query,
    attn_key,
    attn_value,
    attn_out_grad,
):
    seq_count = lax.axis_size("seq")
    seq_index = lax.axis_index("seq")
    local_heads = beta_weight.shape[0]
    beta_logit = jnp.dot(layer_input, beta_weight.T, preferred_element_type=jnp.float32)
    decay_input = jnp.dot(layer_input, decay_weight.T, preferred_element_type=jnp.float32)
    (betas, decays), pull_gate = jax.vjp(gate_values, beta_logit, decay_input, log_rate, decay_bias)
    queries = heads_first(delta_query.astype(jnp.float32), local_heads)
    key_rows = heads_first(delta_key.astype(jnp.float32), local_heads)
    value_rows = heads_first(delta_value.astype(jnp.float32), local_heads)
    out_grad = heads_first(delta_out_grad.astype(jnp.float32), local_heads)
    beta_rows = betas.T
    decay_rows = decays.T
    key_width = key_rows.shape[2]
    identity_mat = jnp.broadcast_to(
        jnp.eye(key_width, dtype=jnp.float32), (local_heads, key_width, key_width)
    )
    zero_mem = jnp.zeros_like(state_init)
    transit = block_forward(
        identity_mat, queries, key_rows, jnp.zeros_like(key_rows), beta_rows, decay_rows
    )[1]
    transit_t = jnp.swapaxes(transit, 1, 2)

    def from_memory(memory):
        return block_forward(memory, queries, key_rows, value_rows, beta_rows, decay_rows)

    primal_zero, pull_zero = jax.vjp(from_memory, zero_mem)
    offset = primal_zero[1]
    local_grad = pull_zero((out_grad, zero_mem))[0]
    is_first = seq_index == 0
    is_last = seq_index == seq_count - 1

    def relay_state(iteration, memory):
        arrived = shifted(chain_mul(transit, memory) + offset, "seq", 1)
        return jnp.where(is_first, state_init, arrived)

    def relay_grad(iteration, memory):
        arrived = shifted(chain_mul(transit_t, memory) + local_grad, "seq", -1)
        return jnp.where(is_last, state_grad_next, arrived)

    mem_in = lax.fori_loop(0, seq_count - 1, relay_state, jnp.where(is_first, state_init, zero_mem))
    grad_end = lax.fori_loop(
        0, seq_count - 1, relay_grad, jnp.where(is_last, state_grad_next, zero_mem)
    )
    primal_full, pull_full = jax.vjp(
        block_forward, mem_in, queries, key_rows, value_rows, beta_rows, decay_rows
    )
    grad_in, grad_q, grad_k, grad_v, grad_beta, grad_decay = pull_full((out_grad, grad_end))
    grad_logit_b, grad_logit_d, grad_rate, grad_bias = pull_gate((grad_beta.T, grad_decay.T))
    every_b, every_d = (
        lax.all_gather(grad_logit_b, "head", axis=1, tiled=True),
        lax.all_gather(grad_logit_d, "head", axis=1, tiled=True),
    )
    cols_b, cols_d = (
        lax.all_to_all(beta_weight, "head", split_axis=1, concat_axis=0, tiled=True),
        lax.all_to_all(decay_weight, "head", split_axis=1, concat_axis=0, tiled=True),
    )
    input_grad = dot_high(every_b, cols_b.astype(jnp.float32)) + dot_high(
        every_d, cols_d.astype(jnp.float32)
    )
    input_rows = layer_input.astype(jnp.float32)
    weight_terms = (dot_high(grad_logit_b.T, input_rows), dot_high(grad_logit_d.T, input_rows))
    beta_weight_grad, decay_weight_grad = (
        lax.psum_scatter(weight_terms[0], "seq", scatter_dimension=1, tiled=True),
        lax.psum_scatter(weight_terms[1], "seq", scatter_dimension=1, tiled=True),
    )
    log_rate_grad, decay_bias_grad = lax.psum((grad_rate, grad_bias), "seq")
    tok_len = attn_query.shape[0]
    reach_blocks = min(WINDOW // tok_len, seq_count - 1)
    pair_local = jnp.stack([attn_key, attn_value])
    fetched = []
    for distance in range(1, reach_blocks + 1):
        fetched.append(shifted(pair_local, "seq", distance))
    ordered = [fetched[distance - 1] for distance in range(reach_blocks, 0, -1)] + [pair_local]
    window_pair = jnp.concatenate(ordered, axis=1)
    q_places = seq_index * tok_len + lax.iota(jnp.int32, tok_len)
    k_places = (seq_index - reach_blocks) * tok_len + lax.iota(
        jnp.int32, (reach_blocks + 1) * tok_len
    )
    grad_aq, grad_window_k, grad_window_v = window_grads(
        attn_query, window_pair[0], window_pair[1], attn_out_grad, q_places, k_places
    )
    grad_pairs = jnp.stack([grad_window_k, grad_window_v])
    own_grads = grad_pairs[:, reach_blocks * tok_len :]
    total_grads = own_grads
    for distance in range(1, reach_blocks + 1):
        total_grads = total_grads + shifted(
            grad_pairs[
                :, (reach_blocks - distance) * tok_len : (reach_blocks - distance + 1) * tok_len
            ],
            "seq",
            -distance,
        )
    boundary = grad_in[None]
    return (
        tokens_first(grad_q),
        tokens_first(grad_k),
        tokens_first(grad_v),
        boundary,
        input_grad,
        beta_weight_grad,
        decay_weight_grad,
        log_rate_grad,
        decay_bias_grad,
        grad_aq,
        total_grads[0],
        total_grads[1],
    )


def solution(mesh):
    placed = (
        P("seq", None),
        P("head", None),
        P("head", None),
        P("head"),
        P("head"),
        P("seq", "head"),
        P("seq", "head"),
        P("seq", "head"),
        P("seq", "head"),
        P("head", None, None),
        P("head", None, None),
        P("seq", "head"),
        P("seq", "head"),
        P("seq", "head"),
        P("seq", "head"),
    )
    return jax.shard_map(
        shards,
        mesh=mesh,
        in_specs=placed,
        out_specs=(
            P("seq", "head"),
            P("seq", "head"),
            P("seq", "head"),
            P("seq", "head", None, None),
            P("seq", "head"),
            P("head", "seq"),
            P("head", "seq"),
            P("head"),
            P("head"),
            P("seq", "head"),
            P("seq", "head"),
            P("seq", "head"),
        ),
        check_vma=False,
    )
```

profile of v0, /device:TPU:0, one launch (start us, length us, event | category | flops | bytes accessed | tf_op | source)
XLA Modules:
  0.0 1099.7 jit_solution(14496573111762103416)
XLA Ops:
  26.2 102.0 %while.168 = (s32[]{:T(128)}, f32[8,128,128]{2,1,0:T(8,128)}, f32[2,8,64,1]{2,1,3,0:T(8,128)S(1)}, f32[2,8,64,1]{2,1,3,0:T(8,128)S(1)}, f32[2,8,64,64]{3,2,1,0:T...) while((s32[]{:T(128)}, f32[8,128,128]{2,1,0:T(8,128)}, ...), condition=%wide.region_7.9_spmd.clone.clone, body=%wide.region_5.8_spmd.clone.clone.sunk | while | flops 353652800 | bytes 5958024 | solution.py:88
  30.3 40.7 %custom-call.49 = f32[8,1,64,64]{2,3,1,0:T(8,128)} custom-call(f32[8,1,64,64]{3,2,1,0:T(8,128)} %add_bitcast_fusion.8), custom_call_target="InvertDiagBlocksLowerTriangular" | custom-call | tf_op jit(solution)/shard_map/jvp()/while/body/eval_jaxpr/vmap(jit(_solve_triangular))/triangular_solve/custom-call.1 | solution.py:52
  80.9 40.7 %custom-call.49 = f32[8,1,64,64]{2,3,1,0:T(8,128)} custom-call(f32[8,1,64,64]{3,2,1,0:T(8,128)} %add_bitcast_fusion.8), custom_call_target="InvertDiagBlocksLowerTriangular" | custom-call | tf_op jit(solution)/shard_map/jvp()/while/body/eval_jaxpr/vmap(jit(_solve_triangular))/triangular_solve/custom-call.1 | solution.py:52
  123.2 3.0 convolution_add_fusion.45
  133.5 101.7 %while.167 = (s32[]{:T(128)}, f32[8,128,128]{2,1,0:T(8,128)}, f32[2,8,1,1]{1,3,2,0:T(1,128)S(1)}, f32[2,8,64,128]{3,2,1,0:T(8,128)}, f32[2,8,64,1]{2,1,3,0:T(8,1...) while((s32[]{:T(128)}, f32[8,128,128]{2,1,0:T(8,128)}, ...), condition=%wide.region_9.12_spmd.clone, body=%wide.region_8.11_spmd.clone.sunk | while | flops 403714112 | bytes 7303539 | solution.py:88
  137.6 40.7 %custom-call.48 = f32[8,1,64,64]{2,3,1,0:T(8,128)} custom-call(f32[8,1,64,64]{3,2,1,0:T(8,128)} %fusion.484), custom_call_target="InvertDiagBlocksLowerTriangular" | custom-call | tf_op jit(solution)/shard_map/transpose(jvp())/while/body/eval_jaxpr/vmap(jit(_solve_triangular))/triangular_solve/custom-call.0 | solution.py:52
  188.5 40.7 %custom-call.48 = f32[8,1,64,64]{2,3,1,0:T(8,128)} custom-call(f32[8,1,64,64]{3,2,1,0:T(8,128)} %fusion.484), custom_call_target="InvertDiagBlocksLowerTriangular" | custom-call | tf_op jit(solution)/shard_map/transpose(jvp())/while/body/eval_jaxpr/vmap(jit(_solve_triangular))/triangular_solve/custom-call.0 | solution.py:52
  236.2 95.8 %while.162 = (s32[]{:T(128)}, f32[8,128,128]{2,1,0:T(8,128)}, f32[2,8,64]{2,1,0:T(8,128)S(1)}, f32[2,8,64,128]{3,2,1,0:T(8,128)S(1)}, f32[2,8,64]{2,1,0:T(8,128)S(1)}, /*index=5*/s32[]{:T(128)}, f32[]{:T(128)}) while((s32[]{:T(128)}, f32[8,128,128]{2,1,0:T(8,128)}, f32[2,8,64]{2,1,0:T(8,128)S(1)}, f32[2,8,64,128]{3,2,1,0:T(8,128)S(1)}, ...), condition=%wide.region_3.5_spmd, body=%wide.region_1.4_spmd.sunk | while | flops 302870592 | bytes 8043833 | solution.py:88
  239.9 40.7 %custom-call.44 = f32[8,1,64,64]{2,3,1,0:T(8,128)} custom-call(f32[8,1,64,64]{3,2,1,0:T(8,128)} %fusion.419), custom_call_target="InvertDiagBlocksLowerTriangular" | custom-call | tf_op jit(solution)/shard_map/while/body/eval_jaxpr/vmap(jit(_solve_triangular))/triangular_solve/custom-call.1 | solution.py:52
  287.8 40.7 %custom-call.44 = f32[8,1,64,64]{2,3,1,0:T(8,128)} custom-call(f32[8,1,64,64]{3,2,1,0:T(8,128)} %fusion.419), custom_call_target="InvertDiagBlocksLowerTriangular" | custom-call | tf_op jit(solution)/shard_map/while/body/eval_jaxpr/vmap(jit(_solve_triangular))/triangular_solve/custom-call.1 | solution.py:52
  335.2 127.4 %while.164 = (s32[]{:T(128)}, f32[8,128,128]{2,1,0:T(8,128)S(1)}, pred[]{:T(512)}, f32[8,128,128]{2,1,0:T(8,128)}, f32[8,128,128]{2,1,0:T(8,128)}, /*index=5*/f32[8,128,128]{2,1,0:T(8,128)}, s32[]{:T(128)}) while((s32[]{:T(128)}, f32[8,128,128]{2,1,0:T(8,128)S(1)}, pred[]{:T(512)}, f32[8,128,128]{2,1,0:T(8,128)}, ...), condition=%wide.region_13.16_spmd, body=%wide.region_12.15_spmd.sunk | while | flops 201588736 | bytes 7864466 | solution.py:195
  335.2 2.6 convolution_add_fusion.34
  337.8 3.8 collective-permute-start.1
  341.6 11.4 %collective-permute-done.1 = f32[8,128,128]{2,1,0:T(8,128)S(1)} collective-permute-done((f32[8,128,128]{2,1,0:T(8,128)}, f32[8,128,128]{2,1,0:T(8,128)S(1)}, u32[]{:S(2)}, u32[]{:S(2)}) %collective-permute-start.1) | collective-permute-done | bytes 524320 | tf_op jit(solution)/shard_map/while/body/eval_jaxpr/ppermute | solution.py:19
  355.0 2.6 convolution_add_fusion.34
  357.6 4.3 collective-permute-start.1
  361.9 10.6 collective-permute-done.1
  374.4 2.6 convolution_add_fusion.34
  377.1 4.4 collective-permute-start.1
  381.5 9.7 collective-permute-done.1
  395.7 5.2 collective-permute-start.1
  400.9 8.7 collective-permute-done.1
  411.5 2.6 convolution_add_fusion.34
  414.1 5.2 collective-permute-start.1
  419.4 7.8 collective-permute-done.1
  429.1 2.6 convolution_add_fusion.34
  431.7 5.2 collective-permute-start.1
  436.9 7.0 collective-permute-done.1
  445.8 2.6 convolution_add_fusion.34
  448.4 5.2 collective-permute-start.1
  453.6 7.0 collective-permute-done.1
  470.9 113.4 %while.165 = (s32[]{:T(128)}, f32[8,128,128]{2,1,0:T(8,128)S(1)}, f32[2,8,64,64]{3,2,1,0:T(8,128)}, f32[2,8,128,64]{2,3,1,0:T(8,128)}, f32[2,8,64,64]{3,2,1,0:T(...) while((s32[]{:T(128)}, f32[8,128,128]{2,1,0:T(8,128)S(1)}, ...), condition=%wide.region_16.19_spmd.clone.clone, body=%wide.region_14.18_spmd.clone.clone.sunk | while | flops 454448192 | bytes 34061148 | solution.py:88
  471.7 2.7 bitcast_dynamic-update-slice_fusion.26
  477.9 40.0 %custom-call.45 = f32[8,1,64,64]{2,3,1,0:T(8,128)S(1)} custom-call(f32[8,1,64,64]{3,2,1,0:T(8,128)} %add_bitcast_fusion.6), custom_call_target="InvertDiagBlocksLowerTriangular" | custom-call | tf_op jit(solution)/shard_map/jvp()/while/body/eval_jaxpr/vmap(jit(_solve_triangular))/triangular_solve/custom-call.1 | solution.py:52
  528.4 2.7 bitcast_dynamic-update-slice_fusion.26
  534.6 40.0 %custom-call.45 = f32[8,1,64,64]{2,3,1,0:T(8,128)S(1)} custom-call(f32[8,1,64,64]{3,2,1,0:T(8,128)} %add_bitcast_fusion.6), custom_call_target="InvertDiagBlocksLowerTriangular" | custom-call | tf_op jit(solution)/shard_map/jvp()/while/body/eval_jaxpr/vmap(jit(_solve_triangular))/triangular_solve/custom-call.1 | solution.py:52
  584.4 124.3 %while.163 = (s32[]{:T(128)}, f32[8,128,128]{2,1,0:T(8,128)S(1)}, pred[]{:T(512)}, f32[8,128,128]{2,1,0:T(8,128)}, f32[8,128,128]{2,1,0:T(8,128)}, /*index=5*/f32[8,128,128]{2,1,0:T(8,128)}, s32[]{:T(128)}) while((s32[]{:T(128)}, f32[8,128,128]{2,1,0:T(8,128)S(1)}, pred[]{:T(512)}, f32[8,128,128]{2,1,0:T(8,128)}, ...), condition=%wide.region_11.14_spmd, body=%wide.region_10.13_spmd.sunk | while | flops 201588736 | bytes 7864466 | solution.py:196
  588.3 11.2 %collective-permute-done = f32[8,128,128]{2,1,0:T(8,128)S(1)} collective-permute-done((f32[8,128,128]{2,1,0:T(8,128)}, f32[8,128,128]{2,1,0:T(8,128)S(1)}, u32[]{:S(2)}, u32[]{:S(2)}) %collective-permute-start) | collective-permute-done | bytes 524320 | tf_op jit(solution)/shard_map/while/body/eval_jaxpr/ppermute | solution.py:19
  605.4 11.2 %collective-permute-done = f32[8,128,128]{2,1,0:T(8,128)S(1)} collective-permute-done((f32[8,128,128]{2,1,0:T(8,128)}, f32[8,128,128]{2,1,0:T(8,128)S(1)}, u32[]{:S(2)}, u32[]{:S(2)}) %collective-permute-start) | collective-permute-done | bytes 524320 | tf_op jit(solution)/shard_map/while/body/eval_jaxpr/ppermute | solution.py:19
  618.5 2.6 convolution_add_fusion.33
  622.5 10.9 collective-permute-done
  635.3 2.6 convolution_add_fusion.33
  639.2 11.7 %collective-permute-done = f32[8,128,128]{2,1,0:T(8,128)S(1)} collective-permute-done((f32[8,128,128]{2,1,0:T(8,128)}, f32[8,128,128]{2,1,0:T(8,128)S(1)}, u32[]{:S(2)}, u32[]{:S(2)}) %collective-permute-start) | collective-permute-done | bytes 524320 | tf_op jit(solution)/shard_map/while/body/eval_jaxpr/ppermute | solution.py:19
  656.7 13.0 %collective-permute-done = f32[8,128,128]{2,1,0:T(8,128)S(1)} collective-permute-done((f32[8,128,128]{2,1,0:T(8,128)}, f32[8,128,128]{2,1,0:T(8,128)S(1)}, u32[]{:S(2)}, u32[]{:S(2)}) %collective-permute-start) | collective-permute-done | bytes 524320 | tf_op jit(solution)/shard_map/while/body/eval_jaxpr/ppermute | solution.py:19
  675.6 14.1 %collective-permute-done = f32[8,128,128]{2,1,0:T(8,128)S(1)} collective-permute-done((f32[8,128,128]{2,1,0:T(8,128)}, f32[8,128,128]{2,1,0:T(8,128)S(1)}, u32[]{:S(2)}, u32[]{:S(2)}) %collective-permute-start) | collective-permute-done | bytes 524320 | tf_op jit(solution)/shard_map/while/body/eval_jaxpr/ppermute | solution.py:19
  691.7 2.6 convolution_add_fusion.33
  695.6 11.2 %collective-permute-done = f32[8,128,128]{2,1,0:T(8,128)S(1)} collective-permute-done((f32[8,128,128]{2,1,0:T(8,128)}, f32[8,128,128]{2,1,0:T(8,128)S(1)}, u32[]{:S(2)}, u32[]{:S(2)}) %collective-permute-start) | collective-permute-done | bytes 524320 | tf_op jit(solution)/shard_map/while/body/eval_jaxpr/ppermute | solution.py:19
  711.2 227.8 %while.166 = (s32[]{:T(128)}, f32[8,128,128]{2,1,0:T(8,128)S(1)}, f32[2,8,64,128]{3,2,0,1:T(8,128)}, f32[2,8,64,128]{3,2,0,1:T(8,128)}, f32[2,8,64,128]{3,2,0,1:...) while((s32[]{:T(128)}, f32[8,128,128]{2,1,0:T(8,128)S(1)}, ...), condition=%wide.region_28.31_spmd.clone.clone, body=%wide.region_17.30_spmd.clone.clone.sunk | while | flops 1034926656 | bytes 50256772 | solution.py:88
  716.8 40.0 %custom-call.47 = f32[8,1,64,64]{2,3,1,0:T(8,128)} custom-call(f32[8,1,64,64]{3,2,1,0:T(8,128)S(1)} %add_bitcast_fusion.7), custom_call_target="InvertDiagBlocksLowerTriangular" | custom-call | tf_op jit(solution)/shard_map/transpose(jvp())/while/body/eval_jaxpr/vmap(jit(_solve_triangular))/triangular_solve | solution.py:52
  762.0 40.7 %custom-call.46 = f32[8,1,64,64]{2,3,1,0:T(8,128)} custom-call(f32[8,1,64,64]{3,2,1,0:T(8,128)} %fusion.459), custom_call_target="InvertDiagBlocksLowerTriangular" | custom-call | tf_op jit(solution)/shard_map/transpose(jvp())/while/body/eval_jaxpr/vmap(jit(_solve_triangular))/triangular_solve/custom-call.0 | solution.py:52
  830.5 40.0 %custom-call.47 = f32[8,1,64,64]{2,3,1,0:T(8,128)} custom-call(f32[8,1,64,64]{3,2,1,0:T(8,128)S(1)} %add_bitcast_fusion.7), custom_call_target="InvertDiagBlocksLowerTriangular" | custom-call | tf_op jit(solution)/shard_map/transpose(jvp())/while/body/eval_jaxpr/vmap(jit(_solve_triangular))/triangular_solve | solution.py:52
  875.7 40.7 %custom-call.46 = f32[8,1,64,64]{2,3,1,0:T(8,128)} custom-call(f32[8,1,64,64]{3,2,1,0:T(8,128)} %fusion.459), custom_call_target="InvertDiagBlocksLowerTriangular" | custom-call | tf_op jit(solution)/shard_map/transpose(jvp())/while/body/eval_jaxpr/vmap(jit(_solve_triangular))/triangular_solve/custom-call.0 | solution.py:52
  943.1 6.2 collective-permute-start.2
  957.4 3.9 all-to-all-start
  970.0 18.6 %all-reduce.2 = (f32[8]{0:T(128)}, f32[8]{0:T(128)}) all-reduce(f32[8]{0:T(128)S(1)} %negate_multiply_fusion, f32[8]{0:T(128)} %get-tuple-element.2915), channel_id=1, replica_groups=mesh['seq'=8,'head'=4] {'seq'}, use_global_device_ids=true, to_apply=%region_34.37 | all-reduce | flops 16 | bytes 128 | tf_op jit(solution)/shard_map/psum | solution.py:221
  996.4 5.2 all_gather.6
  1001.6 5.3 all_gather.7
  1006.9 3.3 all-to-all-start.1
  1015.0 3.1 collective-permute-start.8
  1037.0 2.9 convolution_add_fusion.16
  1046.4 6.3 collective-permute-done.11
  1055.4 26.8 %collective-permute-done.12 = f32[2,128,256]{2,1,0:T(8,128)} collective-permute-done((f32[2,128,256]{2,1,0:T(8,128)}, f32[2,128,256]{2,1,0:T(8,128)}, u32[]{:S(2)}, u32[]{:S(2)}) %collective-permute-start.12) | collective-permute-done | bytes 262176 | tf_op jit(solution)/shard_map/ppermute | solution.py:19
  1082.3 3.8 collective-permute-done.13
  1086.1 4.2 collective-permute-done.9
  (598 shorter events, 295.8 us)
Async XLA Ops:
  7.2 6.6 copy-start
  7.2 1085.3 %reduce-scatter.5.cloned.1.call-start = ((), (), s32[]{:S(2)}) async-start(), calls=%async_computation.5 | async-start | bytes 294912 | tf_op jit(solution)/shard_map/reduce_scatter | solution.py:219
  17.6 7.7 copy-start.52
  137.6 46.6 %copy-start.46 = (f32[2,8,64,1]{2,1,3,0:T(8,128)S(1)}, f32[2,8,64,1]{2,1,3,0:T(8,128)}, u32[]{:S(2)}) copy-start(f32[2,8,64,1]{2,1,3,0:T(8,128)} %copy-done.45) | copy-start | bytes 12292 | tf_op jit(solution)/shard_map/transpose(jvp())/while
  137.6 46.6 %copy-start.67 = (f32[2,8,1,1]{1,3,2,0:T(1,128)S(1)}, f32[2,8,1,1]{1,3,2,0:T(1,128)}, u32[]{:S(2)}) copy-start(f32[2,8,1,1]{1,3,2,0:T(1,128)} %copy-done.66) | copy-start | bytes 196 | tf_op jit(solution)/shard_map/transpose(jvp())/while
  188.5 46.7 %copy-start.46 = (f32[2,8,64,1]{2,1,3,0:T(8,128)S(1)}, f32[2,8,64,1]{2,1,3,0:T(8,128)}, u32[]{:S(2)}) copy-start(f32[2,8,64,1]{2,1,3,0:T(8,128)} %copy-done.45) | copy-start | bytes 12292 | tf_op jit(solution)/shard_map/transpose(jvp())/while
  188.5 46.7 %copy-start.67 = (f32[2,8,1,1]{1,3,2,0:T(1,128)S(1)}, f32[2,8,1,1]{1,3,2,0:T(1,128)}, u32[]{:S(2)}) copy-start(f32[2,8,1,1]{1,3,2,0:T(1,128)} %copy-done.66) | copy-start | bytes 196 | tf_op jit(solution)/shard_map/transpose(jvp())/while
  238.5 43.7 %copy-start.4 = (f32[8,128,128]{2,1,0:T(8,128)S(1)}, f32[8,128,128]{2,1,0:T(8,128)}, u32[]{:S(2)}) copy-start(f32[8,128,128]{2,1,0:T(8,128)} %get-tuple-element.3774) | copy-start | bytes 1572868 | tf_op jit(solution)/shard_map/while
  286.4 43.7 %copy-start.4 = (f32[8,128,128]{2,1,0:T(8,128)S(1)}, f32[8,128,128]{2,1,0:T(8,128)}, u32[]{:S(2)}) copy-start(f32[8,128,128]{2,1,0:T(8,128)} %get-tuple-element.3774) | copy-start | bytes 1572868 | tf_op jit(solution)/shard_map/while
  337.8 15.3 %collective-permute-start.1 = (f32[8,128,128]{2,1,0:T(8,128)}, f32[8,128,128]{2,1,0:T(8,128)S(1)}, u32[]{:S(2)}, u32[]{:S(2)}) collective-permute-start(f32[8,128,128]{2,1,0:T(8,128)} %convolution_add_fusion.34), channel_id=1, source_target_pairs={{0,4},{4,8},{8,12},{12,16},{16,20},{20,24},{24,28},{1,5},{5,9},{9,... | collective-permute-start | bytes 1572872 | tf_op jit(solution)/shard_map/while/body/eval_jaxpr/ppermute | solution.py:19
  357.6 14.9 %collective-permute-start.1 = (f32[8,128,128]{2,1,0:T(8,128)}, f32[8,128,128]{2,1,0:T(8,128)S(1)}, u32[]{:S(2)}, u32[]{:S(2)}) collective-permute-start(f32[8,128,128]{2,1,0:T(8,128)} %convolution_add_fusion.34), channel_id=1, source_target_pairs={{0,4},{4,8},{8,12},{12,16},{16,20},{20,24},{24,28},{1,5},{5,9},{9,... | collective-permute-start | bytes 1572872 | tf_op jit(solution)/shard_map/while/body/eval_jaxpr/ppermute | solution.py:19
  377.1 14.0 %collective-permute-start.1 = (f32[8,128,128]{2,1,0:T(8,128)}, f32[8,128,128]{2,1,0:T(8,128)S(1)}, u32[]{:S(2)}, u32[]{:S(2)}) collective-permute-start(f32[8,128,128]{2,1,0:T(8,128)} %convolution_add_fusion.34), channel_id=1, source_target_pairs={{0,4},{4,8},{8,12},{12,16},{16,20},{20,24},{24,28},{1,5},{5,9},{9,... | collective-permute-start | bytes 1572872 | tf_op jit(solution)/shard_map/while/body/eval_jaxpr/ppermute | solution.py:19
  395.7 13.9 %collective-permute-start.1 = (f32[8,128,128]{2,1,0:T(8,128)}, f32[8,128,128]{2,1,0:T(8,128)S(1)}, u32[]{:S(2)}, u32[]{:S(2)}) collective-permute-start(f32[8,128,128]{2,1,0:T(8,128)} %convolution_add_fusion.34), channel_id=1, source_target_pairs={{0,4},{4,8},{8,12},{12,16},{16,20},{20,24},{24,28},{1,5},{5,9},{9,... | collective-permute-start | bytes 1572872 | tf_op jit(solution)/shard_map/while/body/eval_jaxpr/ppermute | solution.py:19
  414.1 13.0 %collective-permute-start.1 = (f32[8,128,128]{2,1,0:T(8,128)}, f32[8,128,128]{2,1,0:T(8,128)S(1)}, u32[]{:S(2)}, u32[]{:S(2)}) collective-permute-start(f32[8,128,128]{2,1,0:T(8,128)} %convolution_add_fusion.34), channel_id=1, source_target_pairs={{0,4},{4,8},{8,12},{12,16},{16,20},{20,24},{24,28},{1,5},{5,9},{9,... | collective-permute-start | bytes 1572872 | tf_op jit(solution)/shard_map/while/body/eval_jaxpr/ppermute | solution.py:19
  431.7 12.2 %collective-permute-start.1 = (f32[8,128,128]{2,1,0:T(8,128)}, f32[8,128,128]{2,1,0:T(8,128)S(1)}, u32[]{:S(2)}, u32[]{:S(2)}) collective-permute-start(f32[8,128,128]{2,1,0:T(8,128)} %convolution_add_fusion.34), channel_id=1, source_target_pairs={{0,4},{4,8},{8,12},{12,16},{16,20},{20,24},{24,28},{1,5},{5,9},{9,... | collective-permute-start | bytes 1572872 | tf_op jit(solution)/shard_map/while/body/eval_jaxpr/ppermute | solution.py:19
  448.4 12.2 %collective-permute-start.1 = (f32[8,128,128]{2,1,0:T(8,128)}, f32[8,128,128]{2,1,0:T(8,128)S(1)}, u32[]{:S(2)}, u32[]{:S(2)}) collective-permute-start(f32[8,128,128]{2,1,0:T(8,128)} %convolution_add_fusion.34), channel_id=1, source_target_pairs={{0,4},{4,8},{8,12},{12,16},{16,20},{20,24},{24,28},{1,5},{5,9},{9,... | collective-permute-start | bytes 1572872 | tf_op jit(solution)/shard_map/while/body/eval_jaxpr/ppermute | solution.py:19
  470.9 113.4 %copy-start.63 = (s32[64]{0:T(128)S(1)}, s32[64]{0:T(128)}, u32[]{:S(2)}) copy-start(s32[64]{0:T(128)} %iota_add_fusion.7) | copy-start | bytes 772
  518.0 4.9 copy-start.10
  574.7 4.9 copy-start.10
  587.0 12.5 %collective-permute-start = (f32[8,128,128]{2,1,0:T(8,128)}, f32[8,128,128]{2,1,0:T(8,128)S(1)}, u32[]{:S(2)}, u32[]{:S(2)}) collective-permute-start(f32[8,128,128]{2,1,0:T(8,128)} %convolution_add_fusion.33), channel_id=1, source_target_pairs={{4,0},{8,4},{12,8},{16,12},{20,16},{24,20},{28,24},{5,1},{9,5},{13... | collective-permute-start | bytes 1572872 | tf_op jit(solution)/shard_map/while/body/eval_jaxpr/ppermute | solution.py:19
  604.1 12.5 %collective-permute-start = (f32[8,128,128]{2,1,0:T(8,128)}, f32[8,128,128]{2,1,0:T(8,128)S(1)}, u32[]{:S(2)}, u32[]{:S(2)}) collective-permute-start(f32[8,128,128]{2,1,0:T(8,128)} %convolution_add_fusion.33), channel_id=1, source_target_pairs={{4,0},{8,4},{12,8},{16,12},{20,16},{24,20},{28,24},{5,1},{9,5},{13... | collective-permute-start | bytes 1572872 | tf_op jit(solution)/shard_map/while/body/eval_jaxpr/ppermute | solution.py:19
  621.2 12.2 %collective-permute-start = (f32[8,128,128]{2,1,0:T(8,128)}, f32[8,128,128]{2,1,0:T(8,128)S(1)}, u32[]{:S(2)}, u32[]{:S(2)}) collective-permute-start(f32[8,128,128]{2,1,0:T(8,128)} %convolution_add_fusion.33), channel_id=1, source_target_pairs={{4,0},{8,4},{12,8},{16,12},{20,16},{24,20},{28,24},{5,1},{9,5},{13... | collective-permute-start | bytes 1572872 | tf_op jit(solution)/shard_map/while/body/eval_jaxpr/ppermute | solution.py:19
  637.9 13.0 %collective-permute-start = (f32[8,128,128]{2,1,0:T(8,128)}, f32[8,128,128]{2,1,0:T(8,128)S(1)}, u32[]{:S(2)}, u32[]{:S(2)}) collective-permute-start(f32[8,128,128]{2,1,0:T(8,128)} %convolution_add_fusion.33), channel_id=1, source_target_pairs={{4,0},{8,4},{12,8},{16,12},{20,16},{24,20},{28,24},{5,1},{9,5},{13... | collective-permute-start | bytes 1572872 | tf_op jit(solution)/shard_map/while/body/eval_jaxpr/ppermute | solution.py:19
  655.4 14.3 %collective-permute-start = (f32[8,128,128]{2,1,0:T(8,128)}, f32[8,128,128]{2,1,0:T(8,128)S(1)}, u32[]{:S(2)}, u32[]{:S(2)}) collective-permute-start(f32[8,128,128]{2,1,0:T(8,128)} %convolution_add_fusion.33), channel_id=1, source_target_pairs={{4,0},{8,4},{12,8},{16,12},{20,16},{24,20},{28,24},{5,1},{9,5},{13... | collective-permute-start | bytes 1572872 | tf_op jit(solution)/shard_map/while/body/eval_jaxpr/ppermute | solution.py:19
  674.3 15.4 %collective-permute-start = (f32[8,128,128]{2,1,0:T(8,128)}, f32[8,128,128]{2,1,0:T(8,128)S(1)}, u32[]{:S(2)}, u32[]{:S(2)}) collective-permute-start(f32[8,128,128]{2,1,0:T(8,128)} %convolution_add_fusion.33), channel_id=1, source_target_pairs={{4,0},{8,4},{12,8},{16,12},{20,16},{24,20},{28,24},{5,1},{9,5},{13... | collective-permute-start | bytes 1572872 | tf_op jit(solution)/shard_map/while/body/eval_jaxpr/ppermute | solution.py:19
  694.3 12.5 %collective-permute-start = (f32[8,128,128]{2,1,0:T(8,128)}, f32[8,128,128]{2,1,0:T(8,128)S(1)}, u32[]{:S(2)}, u32[]{:S(2)}) collective-permute-start(f32[8,128,128]{2,1,0:T(8,128)} %convolution_add_fusion.33), channel_id=1, source_target_pairs={{4,0},{8,4},{12,8},{16,12},{20,16},{24,20},{28,24},{5,1},{9,5},{13... | collective-permute-start | bytes 1572872 | tf_op jit(solution)/shard_map/while/body/eval_jaxpr/ppermute | solution.py:19
  711.2 228.0 %copy-start.60 = (f32[128,8]{0,1:T(8,128)S(1)}, f32[128,8]{0,1:T(8,128)}, u32[]{:S(2)}) copy-start(f32[128,8]{0,1:T(8,128)} %get-tuple-element.2988) | copy-start | bytes 12292
  711.2 228.0 %copy-start.62 = (f32[8]{0:T(128)S(1)}, f32[8]{0:T(128)}, u32[]{:S(2)}) copy-start(f32[8]{0:T(128)} %copy-done.61) | copy-start | bytes 100
  711.5 5.3 copy-start.19
  802.6 4.5 copy-start.18
  811.7 5.7 copy-start.42
  813.6 5.9 copy-start.3
  813.6 5.9 copy-start.7
  816.0 4.6 copy-start.9
  825.2 5.3 copy-start.19
  916.3 4.5 copy-start.18
  925.4 5.7 copy-start.42
  927.3 5.9 copy-start.3
  927.3 5.9 copy-start.7
  929.7 4.6 copy-start.9
  939.1 24.0 %copy-start.1 = (f32[8,128,128]{2,1,0:T(8,128)}, f32[8,128,128]{2,1,0:T(8,128)S(1)}, u32[]{:S(2)}) copy-start(f32[8,128,128]{2,1,0:T(8,128)S(1)} %get-tuple-element.1901) | copy-start | bytes 1572868
  939.1 22.3 %copy-start.53 = (f32[128,8]{0,1:T(8,128)S(1)}, f32[128,8]{0,1:T(8,128)}, u32[]{:S(2)}) copy-start(f32[128,8]{0,1:T(8,128)} %copy-done.52) | copy-start | bytes 12292
  942.4 22.6 %copy-start.27 = (bf16[128,1024]{0,1:T(8,128)(2,1)S(1)}, bf16[128,1024]{0,1:T(8,128)(2,1)}, u32[]{:S(2)}) copy-start(bf16[128,1024]{0,1:T(8,128)(2,1)} %copy-done.26) | copy-start | bytes 786436
  943.1 69.6 %collective-permute-start.2 = (bf16[2,128,256]{1,2,0:T(8,128)(2,1)}, bf16[2,128,256]{1,2,0:T(8,128)(2,1)}, u32[]{:S(2)}, u32[]{:S(2)}) collective-permute-start(bf16[2,128,256]{1,2,0:T(8,128)(2,1)} %pad_maximum_fusion.1), channel_id=1, source_target_pairs={{0,28},{1,29},{2,30},{3,31}} | collective-permute-start | bytes 393224 | tf_op jit(solution)/shard_map/ppermute | solution.py:19
  949.3 65.6 %collective-permute-start.3 = (bf16[2,128,256]{1,2,0:T(8,128)(2,1)}, bf16[2,128,256]{1,2,0:T(8,128)(2,1)}, u32[]{:S(2)}, u32[]{:S(2)}) collective-permute-start(bf16[2,128,256]{1,2,0:T(8,128)(2,1)} %pad_maximum_fusion.1), channel_id=1, source_target_pairs={{0,24},{4,28},{1,25},{5,29},{2,26},{6,30},{3,27},{7,31}} | collective-permute-start | bytes 393224 | tf_op jit(solution)/shard_map/ppermute | solution.py:19
  951.6 67.5 %collective-permute-start.4 = (bf16[2,128,256]{1,2,0:T(8,128)(2,1)}, bf16[2,128,256]{1,2,0:T(8,128)(2,1)}, u32[]{:S(2)}, u32[]{:S(2)}) collective-permute-start(bf16[2,128,256]{1,2,0:T(8,128)(2,1)} %pad_maximum_fusion.1), channel_id=1, source_target_pairs={{0,20},{4,24},{8,28},{1,21},{5,25},{9,29},{2,22},{6,26},{10,30},{3... | collective-permute-start | bytes 393224 | tf_op jit(solution)/shard_map/ppermute | solution.py:19
  953.5 66.5 %collective-permute-start.5 = (bf16[2,128,256]{1,2,0:T(8,128)(2,1)}, bf16[2,128,256]{1,2,0:T(8,128)(2,1)}, u32[]{:S(2)}, u32[]{:S(2)}) collective-permute-start(bf16[2,128,256]{1,2,0:T(8,128)(2,1)} %pad_maximum_fusion.1), channel_id=1, source_target_pairs={{0,16},{4,20},{8,24},{12,28},{1,17},{5,21},{9,25},{13,29},{2,18},{... | collective-permute-start | bytes 393224 | tf_op jit(solution)/shard_map/ppermute | solution.py:19
  955.4 65.5 %collective-permute-start.6 = (bf16[2,128,256]{1,2,0:T(8,128)(2,1)}, bf16[2,128,256]{1,2,0:T(8,128)(2,1)}, u32[]{:S(2)}, u32[]{:S(2)}) collective-permute-start(bf16[2,128,256]{1,2,0:T(8,128)(2,1)} %pad_maximum_fusion.1), channel_id=1, source_target_pairs={{0,12},{4,16},{8,20},{12,24},{16,28},{1,13},{5,17},{9,21},{13,25},... | collective-permute-start | bytes 393224 | tf_op jit(solution)/shard_map/ppermute | solution.py:19
  957.4 49.5 %all-to-all-start = ((bf16[8,4,2048]{2,0,1:T(8,128)(2,1)}), bf16[8,4,2048]{2,0,1:T(8,128)(2,1)}, u32[]{:S(2)}, u32[]{:S(2)}) async-start(bf16[8,4,2048]{2,0,1:T(8,128)(2,1)} %bitcast.49), calls=%async_computation | async-start | bytes 262144 | tf_op jit(solution)/shard_map/all_to_all | solution.py:209
  961.3 131.1 %reduce-scatter.3.cloned.1.call-start = ((), (), s32[]{:S(2)}) async-start(), calls=%async_computation.4 | async-start | bytes 294912 | tf_op jit(solution)/shard_map/reduce_scatter | solution.py:218
  966.0 25.1 %copy-start.39 = (f32[8,128,128]{1,2,0:T(8,128)S(1)}, f32[8,128,128]{1,2,0:T(8,128)}, u32[]{:S(2)}) copy-start(f32[8,128,128]{1,2,0:T(8,128)} %add_add_fusion) | copy-start | bytes 1572868
  991.1 10.4 copy-start.55
  1006.9 30.1 %all-to-all-start.1 = ((bf16[8,4,2048]{2,0,1:T(8,128)(2,1)}), bf16[8,4,2048]{2,0,1:T(8,128)(2,1)S(1)}, u32[]{:S(2)}, u32[]{:S(2)}) async-start(bf16[8,4,2048]{2,0,1:T(8,128)(2,1)} %bitcast.54), calls=%async_computation.1 | async-start | bytes 262144 | tf_op jit(solution)/shard_map/all_to_all | solution.py:210
  1012.7 9.2 collective-permute-start.7
  1015.0 7.0 collective-permute-start.8
  1034.4 10.7 collective-permute-start.10
  1035.7 17.0 %collective-permute-start.11 = (f32[2,128,256]{2,1,0:T(8,128)}, f32[2,128,256]{2,1,0:T(8,128)}, u32[]{:S(2)}, u32[]{:S(2)}) collective-permute-start(f32[2,128,256]{2,1,0:T(8,128)} %get-tuple-element.2975), channel_id=1, source_target_pairs={{12,0},{16,4},{20,8},{24,12},{28,16},{13,1},{17,5},{21,9},{25,13},... | collective-permute-start | bytes 786440 | tf_op jit(solution)/shard_map/ppermute | solution.py:19
  1037.0 17.0 %copy-start.32 = (bf16[1,1024,256]{1,2,0:T(8,128)(2,1)S(1)}, bf16[1,1024,256]{1,2,0:T(8,128)(2,1)}, u32[]{:S(2)}) copy-start(bf16[1,1024,256]{1,2,0:T(8,128)(2,1)} %copy-done.31) | copy-start | bytes 1572868
  1037.0 17.0 %copy-start.34 = (f32[2,128,1024]{1,2,0:T(8,128)S(1)}, f32[2,128,1024]{1,2,0:T(8,128)}, u32[]{:S(2)}) copy-start(f32[2,128,1024]{1,2,0:T(8,128)} %copy-done.33) | copy-start | bytes 3145732
  1040.0 42.3 %collective-permute-start.12 = (f32[2,128,256]{2,1,0:T(8,128)}, f32[2,128,256]{2,1,0:T(8,128)}, u32[]{:S(2)}, u32[]{:S(2)}) collective-permute-start(f32[2,128,256]{2,1,0:T(8,128)} %get-tuple-element.2976), channel_id=1, source_target_pairs={{16,0},{20,4},{24,8},{28,12},{17,1},{21,5},{25,9},{29,13},{18,2},{... | collective-permute-start | bytes 786440 | tf_op jit(solution)/shard_map/ppermute | solution.py:19
  1041.2 44.8 %collective-permute-start.13 = (f32[2,128,256]{2,1,0:T(8,128)}, f32[2,128,256]{2,1,0:T(8,128)}, u32[]{:S(2)}, u32[]{:S(2)}) collective-permute-start(f32[2,128,256]{2,1,0:T(8,128)} %get-tuple-element.2977), channel_id=1, source_target_pairs={{20,0},{24,4},{28,8},{21,1},{25,5},{29,9},{22,2},{26,6},{30,10},{2... | collective-permute-start | bytes 786440 | tf_op jit(solution)/shard_map/ppermute | solution.py:19
  1042.5 43.5 %collective-permute-start.14 = (f32[2,128,256]{2,1,0:T(8,128)}, f32[2,128,256]{2,1,0:T(8,128)}, u32[]{:S(2)}, u32[]{:S(2)}) collective-permute-start(f32[2,128,256]{2,1,0:T(8,128)} %get-tuple-element.2979), channel_id=1, source_target_pairs={{24,0},{28,4},{25,1},{29,5},{26,2},{30,6},{27,3},{31,7}} | collective-permute-start | bytes 786440 | tf_op jit(solution)/shard_map/ppermute | solution.py:19
  1045.1 41.0 %collective-permute-start.15 = (f32[2,128,256]{2,1,0:T(8,128)}, f32[2,128,256]{2,1,0:T(8,128)}, u32[]{:S(2)}, u32[]{:S(2)}) collective-permute-start(f32[2,128,256]{2,1,0:T(8,128)} %get-tuple-element.2978), channel_id=1, source_target_pairs={{28,0},{29,1},{30,2},{31,3}} | collective-permute-start | bytes 786440 | tf_op jit(solution)/shard_map/ppermute | solution.py:19
  1052.7 37.5 %collective-permute-start.9 = (f32[2,128,256]{2,1,0:T(8,128)}, f32[2,128,256]{2,1,0:T(8,128)}, u32[]{:S(2)}, u32[]{:S(2)}) collective-permute-start(f32[2,128,256]{2,1,0:T(8,128)} %get-tuple-element.2973), channel_id=1, source_target_pairs={{4,0},{8,4},{12,8},{16,12},{20,16},{24,20},{28,24},{5,1},{9,5},{13... | collective-permute-start | bytes 786440 | tf_op jit(solution)/shard_map/ppermute | solution.py:19
  (81 other events, 185.7 us)
Sparse Core Ops, SparseCore 0:
  942.3 64.0 reduce-scatter.4
  1010.3 71.9 reduce-scatter.2
where the time goes:
time: 1110 us; the launch traced here: 1100 us
  other arithmetic  535 us (48%)
  waiting for transfers between devices  188 us (17%)
  matrix products  169 us (15%)
  local copies, waits for them, and re-layouts  84.2 us (8%)
  starting transfers between devices  77.2 us (7%)
  blocking collectives  29.1 us (3%)
  between operations  15.4 us (1%)
    another operation x46, other arithmetic, stretch_step(): jax.scipy.linalg.solve_triangular(system_mat, right_side, lower=True, uni...  493 us
    ppermute x28, waiting for transfers between devices, shifted(): return lax.ppermute(value, axis, pairs)  188 us
    dot_general x60, matrix products, dot_high(): return jnp.matmul(left_mat, right_mat, precision=PRECISE)  98.2 us
    ppermute x28, starting transfers between devices, shifted(): return lax.ppermute(value, axis, pairs)  69.9 us
    dot_general x14, matrix products, chain_mul(): return jnp.einsum('hij,hjk->hik', left_mat, right_mat, precision=PRECISE)  37 us
  transfers between devices with their start and end apart: 32, of which 19 were waited for; matrix products, arithmetic and copies ran while one was open for 4% of the time, Pallas kernels for 0%

commit v1 on v0

v1 whole, which is shorter than its diff:
```python
import functools
import math

import jax
import jax.numpy as jnp
from jax import lax
from jax.experimental import pallas as pl
from jax.experimental.pallas import tpu as pltpu
from jax.sharding import PartitionSpec as P

AHD = 128
WINDOW = 1024
HOP_TICKS = 3
MESH = pl.DeviceIdType.MESH
PRECISE = lax.Precision.HIGHEST
F32 = jnp.float32
BF16 = jnp.bfloat16
NN = (((1,), (0,)), ((), ()))
NT = (((1,), (1,)), ((), ()))
TN = (((0,), (0,)), ((), ()))


def parts(value):
    if isinstance(value, tuple):
        return value
    if value.dtype == BF16:
        return (value,)
    high = value.astype(BF16)
    return (high, (value - high.astype(F32)).astype(BF16))


def mul(left, right, dims=NN):
    left, right = parts(left), parts(right)
    total = None
    for i, a in reversed(list(enumerate(left))):
        for j, b in reversed(list(enumerate(right))):
            if i + j < 2:
                term = lax.dot_general(a, b, dims, preferred_element_type=F32)
                total = term if total is None else total + term
    return total


def row_sum(value):
    return jnp.sum(value, axis=1, keepdims=True)


def col_sum(value):
    return jnp.sum(value, axis=0, keepdims=True)


def grids(size):
    rows = lax.broadcasted_iota(jnp.int32, (size, size), 0)
    cols = lax.broadcasted_iota(jnp.int32, (size, size), 1)
    return rows, cols


def as_row(col, rows, cols):
    return col_sum(jnp.where(rows == cols, col, 0.0))


def head_terms(q, k, decay, rows, cols):
    kf = k.astype(F32)
    qf = q.astype(F32)
    k_norm = lax.rsqrt(row_sum(kf * kf) + 1e-06)
    q_norm = lax.rsqrt(row_sum(qf * qf) + 1e-06)
    rk = k_norm
    rq = q_norm * (1.0 / math.sqrt(q.shape[1]))
    decay_row = as_row(decay, rows, cols)
    cum = row_sum(jnp.where(cols <= rows, decay_row, 0.0))
    cum_row = as_row(cum, rows, cols)
    lower = rows >= cols
    ratios = jnp.where(lower, jnp.exp(jnp.where(lower, cum - cum_row, 0.0)), 0.0)
    growth = jnp.exp(cum)
    last = row_sum(decay_row)
    tail = jnp.exp(last - cum)
    return kf, qf, k_norm, q_norm, rk, rq, ratios, growth, jnp.exp(last), tail


def local_kernel(q_ref, k_ref, v_ref, do_ref, beta_ref, decay_ref,
                 transit_ref, offset_ref, lgrad_ref, t_ref, w_ref, uv_ref, p_ref, n_ref):
    size = q_ref.shape[0]
    count = beta_ref.shape[2]
    width = q_ref.shape[1] // count
    rows, cols = grids(size)
    inverses, systems, kept = [], [], []
    for j in range(count):
        lanes = slice(j * width, (j + 1) * width)
        q, k = q_ref[:, lanes], k_ref[:, lanes]
        beta, decay = beta_ref[0, :, j:j + 1], decay_ref[0, :, j:j + 1]
        kf, qf, _, _, rk, rq, ratios, growth, last, tail = head_terms(q, k, decay, rows, cols)
        rk_row = as_row(rk, rows, cols)
        near = jnp.where(rows > cols, ratios * (mul(k, k, NT) * rk * rk_row), 0.0)
        mixing = ratios * (mul(q, k, NT) * rq * rk_row)
        n_ref[j] = near
        p_ref[j] = mixing
        systems.append(beta * near)
        kept.append((kf * rk, qf * rq, beta, growth, last, tail, mixing))
        pair = (rows // 2 == cols // 2) & (rows > cols)
        inverses.append(jnp.where(rows == cols, 1.0, jnp.where(pair, -systems[-1], 0.0)))
    span = 2
    while span < size:
        mask = (rows // (2 * span) == cols // (2 * span)) & (rows // span > cols // span)
        split = [parts(inverse) for inverse in inverses]
        halves = [mul(split[j], jnp.where(mask, systems[j], 0.0)) for j in range(count)]
        inverses = [inverses[j] - mul(halves[j], split[j]) for j in range(count)]
        span *= 2
    for j in range(count):
        lanes = slice(j * width, (j + 1) * width)
        keys, queries, beta, growth, last, tail, mixing = kept[j]
        t_ref[j] = inverses[j]
        split = parts(inverses[j])
        w_all = mul(split, (beta * growth) * keys)
        uv_all = mul(split, beta * v_ref[:, lanes].astype(F32))
        w_ref[j] = w_all
        uv_ref[j] = uv_all
        w_split = parts(w_all)
        tail_keys = parts(keys * tail)
        transit_ref[j] = jnp.where(rows == cols, last, 0.0) - mul(tail_keys, w_split, TN)
        offset_ref[j] = mul(tail_keys, uv_all, TN)
        reach = growth * queries - mul(mixing, w_split)
        lgrad_ref[j] = mul(reach, do_ref[:, lanes], TN)


def relay_kernel(n, transit_ref, offset_ref, lgrad_ref, init_ref, next_ref, mem_ref, grad_ref,
                 send_f, recv_f, send_b, recv_b, sf_sem, rf_sem, sb_sem, rb_sem):
    me = lax.axis_index("seq")
    head = lax.axis_index("head")
    heads = transit_ref.shape[0]
    right, left = lax.rem(me + 1, n), lax.rem(me + n - 1, n)
    has_left, has_right = me > 0, me < n - 1
    barrier = pltpu.get_barrier_semaphore()

    @pl.when(has_left)
    def _():
        pl.semaphore_signal(barrier, inc=1, device_id=(left, head), device_id_type=MESH)

    @pl.when(has_right)
    def _():
        pl.semaphore_signal(barrier, inc=1, device_id=(right, head), device_id_type=MESH)

    pl.semaphore_wait(barrier, has_left.astype(jnp.int32) + has_right.astype(jnp.int32))

    def copy_f(h):
        return pltpu.make_async_remote_copy(
            src_ref=send_f.at[h], dst_ref=recv_f.at[h], send_sem=sf_sem.at[h],
            recv_sem=rf_sem.at[h], device_id=(right, head), device_id_type=MESH)

    def copy_b(h):
        return pltpu.make_async_remote_copy(
            src_ref=send_b.at[h], dst_ref=recv_b.at[h], send_sem=sb_sem.at[h],
            recv_sem=rb_sem.at[h], device_id=(left, head), device_id_type=MESH)

    def tick(t, carry):
        hf = t - HOP_TICKS * me
        hb = t - HOP_TICKS * (n - 1 - me)

        @pl.when((hf >= 0) & (hf < heads))
        def _():
            @pl.when(has_left)
            def _():
                copy_f(hf).wait_recv()
                mem_ref[hf] = recv_f[hf]

            @pl.when(jnp.logical_not(has_left))
            def _():
                mem_ref[hf] = init_ref[hf]

            @pl.when(has_right)
            def _():
                send_f[hf] = mul(transit_ref[hf], mem_ref[hf]) + offset_ref[hf]
                copy_f(hf).start()

        @pl.when((hb >= 0) & (hb < heads))
        def _():
            @pl.when(has_right)
            def _():
                copy_b(hb).wait_recv()
                grad_ref[hb] = recv_b[hb]

            @pl.when(jnp.logical_not(has_right))
            def _():
                grad_ref[hb] = next_ref[hb]

            @pl.when(has_left)
            def _():
                send_b[hb] = mul(transit_ref[hb], grad_ref[hb], TN) + lgrad_ref[hb]
                copy_b(hb).start()

        return carry

    lax.fori_loop(0, HOP_TICKS * (n - 1) + heads, tick, 0)

    def drain(h, carry):
        @pl.when(has_right)
        def _():
            copy_f(h).wait_send()

        @pl.when(has_left)
        def _():
            copy_b(h).wait_send()

        return carry

    lax.fori_loop(0, heads, drain, 0)


def grads_kernel(q_ref, k_ref, v_ref, do_ref, beta_ref, decay_ref, mem_ref, grad_ref,
                 transit_ref, lgrad_ref, t_ref, w_ref, uv_ref, p_ref, n_ref,
                 dq_ref, dk_ref, dv_ref, bound_ref, dbeta_ref, ddecay_ref):
    size = q_ref.shape[0]
    count = beta_ref.shape[2]
    width = q_ref.shape[1] // count
    rows, cols = grids(size)
    for j in range(count):
        lanes = slice(j * width, (j + 1) * width)
        q, k, do = q_ref[:, lanes], k_ref[:, lanes], do_ref[:, lanes]
        beta, decay = beta_ref[0, :, j:j + 1], decay_ref[0, :, j:j + 1]
        kf, qf, k_norm, q_norm, rk, rq, ratios, growth, last, tail = head_terms(
            q, k, decay, rows, cols)
        rk_row = as_row(rk, rows, cols)
        dof = do.astype(F32)
        memory, grad = mem_ref[j], grad_ref[j]
        near, mixing = n_ref[j], p_ref[j]
        mem_s, grad_s = parts(memory), parts(grad)
        updates = uv_ref[j] - mul(w_ref[j], mem_s)
        up_s = parts(updates)
        q_mem = rq * mul(q, mem_s)
        k_mem = rk * mul(k, mem_s)
        dup = mul(mixing, do, TN) + (rk * tail) * mul(k, grad_s)
        drhs = mul(t_ref[j], dup, TN)
        drhs_s = parts(drhs)
        dmix = jnp.where(rows >= cols, mul(do, up_s, NT), 0.0)
        dqk = dmix * ratios
        dsys = jnp.where(rows > cols, -mul(drhs_s, up_s, NT), 0.0)
        dgram = dsys * beta * ratios
        dval = beta * drhs
        dquery = growth * mul(do, mem_s, NT) + mul(dqk * rk_row, k)
        dtail = mul(up_s, grad_s, NT)
        dkey = mul(dqk * rq, q, TN) + dtail * tail
        dkey = dkey - (beta * growth) * mul(drhs_s, mem_s, NT)
        dkey = dkey + mul((dgram + dgram.T) * rk_row, k)
        dbeta = row_sum(drhs * (v_ref[:, lanes].astype(F32) - growth * k_mem))
        dbeta_ref[0, :, j:j + 1] = dbeta + row_sum(dsys * near)
        inner = dsys * (beta * near) + dmix * mixing
        tails = row_sum(dtail * kf) * (rk * tail)
        dcum = growth * (row_sum(dof * q_mem) - row_sum(dval * k_mem)) - tails + row_sum(inner)
        dcum_row = as_row(dcum, rows, cols) - col_sum(inner)
        at_end = col_sum(tails) + last * col_sum(row_sum(grad * memory))
        ddecay_ref[0, :, j:j + 1] = row_sum(jnp.where(cols >= rows, dcum_row, 0.0)) + at_end
        dq_ref[:, lanes] = rq * (dquery - qf * (q_norm * q_norm * row_sum(qf * dquery)))
        dk_ref[:, lanes] = rk * (dkey - kf * (k_norm * k_norm * row_sum(kf * dkey)))
        dv_ref[:, lanes] = dval
        bound_ref[0, j] = mul(transit_ref[j], grad_s, TN) + lgrad_ref[j]


def attn_rows_kernel(start_ref, q_ref, g_ref, k_ref, v_ref, dq_ref, stat_ref):
    size = q_ref.shape[0]
    span = k_ref.shape[0] * k_ref.shape[1]
    scale = 1.0 / math.sqrt(AHD)
    keys = k_ref[...].reshape(span, AHD)
    values = v_ref[...].reshape(span, AHD)
    gap = (start_ref[0] + lax.broadcasted_iota(jnp.int32, (size, span), 0)
           - lax.broadcasted_iota(jnp.int32, (size, span), 1))
    scores = mul(q_ref[...], keys, NT) * scale
    scores = jnp.where((gap >= 0) & (gap < WINDOW), scores, -1e30)
    top = jnp.max(scores, axis=1, keepdims=True)
    weights = jnp.exp(scores - top)
    inverse = 1.0 / row_sum(weights)
    weights = weights * inverse
    weight_grad = mul(g_ref[...], values, NT)
    row_term = row_sum(weights * weight_grad)
    dscores = weights * (weight_grad - row_term) * scale
    dq_ref[...] = mul(dscores, keys)
    stat_ref[0, :, 0:1] = top
    stat_ref[0, :, 1:2] = inverse
    stat_ref[0, :, 2:3] = row_term


def attn_keys_kernel(start_ref, k_ref, v_ref, q_ref, g_ref, stat_ref, dk_ref, dv_ref):
    size = k_ref.shape[0]
    span = q_ref.shape[0] * q_ref.shape[1]
    scale = 1.0 / math.sqrt(AHD)
    queries = q_ref[...].reshape(span, AHD)
    grads = g_ref[...].reshape(span, AHD)
    stats = stat_ref[...].reshape(span, stat_ref.shape[3])
    gap = (start_ref[0] + lax.broadcasted_iota(jnp.int32, (span, size), 0)
           - lax.broadcasted_iota(jnp.int32, (span, size), 1))
    allowed = (gap >= 0) & (gap < WINDOW)
    scores = mul(queries, k_ref[...], NT) * scale
    weights = jnp.where(allowed, jnp.exp(jnp.where(allowed, scores - stats[:, 0:1], 0.0)), 0.0)
    weights = weights * stats[:, 1:2]
    weight_grad = mul(grads, v_ref[...], NT)
    dscores = weights * (weight_grad - stats[:, 2:3]) * scale
    dv_ref[...] = mul(weights, grads, TN)
    dk_ref[...] = mul(dscores, queries, TN)


def attention(attn_query, attn_key, attn_value, attn_out_grad, n, me):
    size, width = attn_query.shape
    heads = width // AHD
    reach = min(-(-WINDOW // size), n - 1)
    span = reach + 1
    gathered = lax.all_gather(
        jnp.concatenate([attn_query, attn_key, attn_value, attn_out_grad], axis=1), "seq")
    first = jnp.clip(me - reach, 0, n - span)
    after = jnp.clip(me, 0, n - span)
    earlier = later = gathered
    if span < n:
        earlier = lax.dynamic_slice_in_dim(gathered, first, span, 0)
        later = lax.dynamic_slice_in_dim(gathered, after, span, 0)

    def own():
        return pl.BlockSpec((size, AHD), lambda h: (0, h))

    def others(group):
        return pl.BlockSpec((span, size, AHD), lambda h: (0, 0, group * heads + h))

    smem = pl.BlockSpec(memory_space=pltpu.SMEM)
    wide = jax.ShapeDtypeStruct((size, width), F32)
    params = pltpu.CompilerParams(vmem_limit_bytes=40 * 1024 * 1024)
    cost = pl.CostEstimate(flops=6 * size * span * size * width, bytes_accessed=8 * span * size * width, transcendentals=size * span * size * heads)
    dquery, stats = pl.pallas_call(
        attn_rows_kernel,
        grid=(heads,),
        out_shape=(wide, jax.ShapeDtypeStruct((heads, size, 3), F32)),
        in_specs=[smem, own(), own(), others(1), others(2)],
        out_specs=(own(), pl.BlockSpec((1, size, 3), lambda h: (h, 0, 0))),
        compiler_params=params, cost_estimate=cost, name="attn_rows",
    )(((me - first) * size).reshape(1).astype(jnp.int32), attn_query, attn_out_grad, earlier, earlier)
    every = lax.all_gather(stats, "seq")
    if span < n:
        every = lax.dynamic_slice_in_dim(every, after, span, 0)
    dkey, dvalue = pl.pallas_call(
        attn_keys_kernel,
        grid=(heads,),
        out_shape=(wide, wide),
        in_specs=[smem, own(), own(), others(0), others(3),
                  pl.BlockSpec((span, 1, size, 3), lambda h: (0, h, 0, 0))],
        out_specs=(own(), own()),
        compiler_params=params, cost_estimate=cost, name="attn_keys",
    )(((after - me) * size).reshape(1).astype(jnp.int32), attn_key, attn_value, later, later, every)
    return dquery, dkey, dvalue


def delta(delta_query, delta_key, delta_value, delta_out_grad, betas, decays,
          state_init, state_grad_next, n):
    size, width = delta_query.shape
    heads = betas.shape[1]
    dim = width // heads
    group = next(c for c in (4, 2, 1) if heads % c == 0)
    steps = heads // group

    def by_step(flat):
        return jnp.swapaxes(flat.reshape(size, steps, group), 0, 1)

    tokens = pl.BlockSpec((size, group * dim), lambda i: (0, i))
    gate = pl.BlockSpec((1, size, group), lambda i: (i, 0, 0))
    square = pl.BlockSpec((group, dim, dim), lambda i: (i, 0, 0))
    pairs = pl.BlockSpec((group, size, size), lambda i: (i, 0, 0))
    token_rows = pl.BlockSpec((group, size, dim), lambda i: (i, 0, 0))
    state = jax.ShapeDtypeStruct((heads, dim, dim), F32)
    pair = jax.ShapeDtypeStruct((heads, size, size), F32)
    per_token = jax.ShapeDtypeStruct((heads, size, dim), F32)
    params = pltpu.CompilerParams(vmem_limit_bytes=48 * 1024 * 1024)
    beta_steps, decay_steps = by_step(betas), by_step(decays)
    flops = 2 * heads * size * size * dim
    transit, offset, lgrad, inverse, w_all, uv_all, mixing, near = pl.pallas_call(
        local_kernel,
        grid=(steps,),
        out_shape=(state, state, state, pair, per_token, per_token, pair, pair),
        in_specs=[tokens] * 4 + [gate] * 2,
        out_specs=(square, square, square, pairs, token_rows, token_rows, pairs, pairs),
        compiler_params=params, name="delta_local",
        cost_estimate=pl.CostEstimate(flops=60 * flops, bytes_accessed=6 << 20, transcendentals=0),
    )(delta_query, delta_key, delta_value, delta_out_grad, beta_steps, decay_steps)
    vmem = pl.BlockSpec(memory_space=pltpu.VMEM)
    sem = pltpu.SemaphoreType.DMA((heads,))
    box = pltpu.VMEM((heads, dim, dim), F32)
    mem_in, grad_end = pl.pallas_call(
        functools.partial(relay_kernel, n),
        out_shape=(state, state),
        in_specs=[vmem] * 5,
        out_specs=(vmem, vmem),
        scratch_shapes=[box, box, box, box, sem, sem, sem, sem],
        compiler_params=pltpu.CompilerParams(
            collective_id=0, has_side_effects=True, vmem_limit_bytes=32 * 1024 * 1024),
        name="state_relay",
        cost_estimate=pl.CostEstimate(flops=6 * flops, bytes_accessed=4 << 20, transcendentals=0),
    )(transit, offset, lgrad, state_init, state_grad_next)
    flat = jax.ShapeDtypeStruct((size, width), F32)
    gate_out = jax.ShapeDtypeStruct((steps, size, group), F32)
    dq, dk, dv, boundary, dbeta, ddecay = pl.pallas_call(
        grads_kernel,
        grid=(steps,),
        out_shape=(flat, flat, flat, jax.ShapeDtypeStruct((1, heads, dim, dim), F32),
                   gate_out, gate_out),
        in_specs=[tokens] * 4 + [gate] * 2 + [square] * 4 + [pairs, token_rows, token_rows, pairs, pairs],
        out_specs=(tokens, tokens, tokens,
                   pl.BlockSpec((1, group, dim, dim), lambda i: (0, i, 0, 0)), gate, gate),
        compiler_params=params, name="delta_grads",
        cost_estimate=pl.CostEstimate(flops=50 * flops, bytes_accessed=9 << 20, transcendentals=0),
    )(delta_query, delta_key, delta_value, delta_out_grad, beta_steps, decay_steps,
      mem_in, grad_end, transit, lgrad, inverse, w_all, uv_all, mixing, near)

    def by_token(stepped):
        return jnp.swapaxes(stepped, 0, 1).reshape(size, heads)

    return dq, dk, dv, boundary, by_token(dbeta), by_token(ddecay)


def dot_high(left_mat, right_mat):
    return jnp.matmul(left_mat, right_mat, precision=PRECISE)


def gate_values(beta_logit, decay_input, log_rate, decay_bias):
    betas = jax.nn.sigmoid(beta_logit)
    decays = -jnp.exp(log_rate)[None, :] * jax.nn.softplus(decay_input + decay_bias[None, :])
    return (betas, decays)


def shards(layer_input, beta_weight, decay_weight, log_rate, decay_bias, delta_query, delta_key,
           delta_value, delta_out_grad, state_init, state_grad_next, attn_query, attn_key,
           attn_value, attn_out_grad):
    n = lax.axis_size("seq")
    me = lax.axis_index("seq")
    heads = beta_weight.shape[0]
    both_weight = jnp.concatenate([beta_weight, decay_weight], axis=0)
    logits = lax.dot_general(layer_input, both_weight, NT, preferred_element_type=F32)
    (betas, decays), pull_gate = jax.vjp(
        gate_values, logits[:, :heads], logits[:, heads:], log_rate, decay_bias)
    cols = lax.all_to_all(both_weight, "head", split_axis=1, concat_axis=0, tiled=True)
    dquery, dkey, dvalue = attention(attn_query, attn_key, attn_value, attn_out_grad, n, me)
    dq, dk, dv, boundary, dbeta, ddecay = delta(
        delta_query, delta_key, delta_value, delta_out_grad, betas, decays,
        state_init, state_grad_next, n)
    grad_b, grad_d, grad_rate, grad_bias = pull_gate((dbeta, ddecay))
    mine = jnp.concatenate([grad_b, grad_d], axis=1)
    every = lax.all_gather(mine, "head", axis=1, tiled=True)
    input_grad = dot_high(every, cols.astype(F32))
    terms = dot_high(mine.T, layer_input.astype(F32))
    weight_grad = lax.psum_scatter(terms, "seq", scatter_dimension=1, tiled=True)
    params = lax.psum(jnp.stack([grad_rate, grad_bias]), "seq")
    return (dq, dk, dv, boundary, input_grad, weight_grad[:heads], weight_grad[heads:],
            params[0], params[1], dquery, dkey, dvalue)


def solution(mesh):
    rows, heads, both = P("seq", None), P("head"), P("seq", "head")
    wide, state = P("head", None), P("head", None, None)
    return jax.shard_map(
        shards,
        mesh=mesh,
        in_specs=(rows, wide, wide, heads, heads, both, both, both, both, state, state,
                  both, both, both, both),
        out_specs=(both, both, both, P("seq", "head", None, None), both, P("head", "seq"),
                   P("head", "seq"), heads, heads, both, both, both),
        check_vma=False,
    )
```

time: 1110 us -> 238 us (0.21)
  other arithmetic: 535 us -> 1.76 us
  matrix products: 169 us -> 3.96 us
  waiting for transfers between devices: 188 us -> 78.6 us
  local copies, waits for them, and re-layouts: 84.2 us -> 9.55 us
  starting transfers between devices: 77.2 us -> 3.5 us
  Pallas kernels: 0 us -> 70.7 us
  blocking collectives: 29.1 us -> 55.3 us
    another operation x63 -> x2, other arithmetic: 498 us -> 0.02 us  [shards(): params = lax.psum(jnp.stack([grad_rate, grad_bias]), 'seq')]
    ppermute x28 -> x0, waiting for transfers between devices: 188 us -> none  [shifted(): return lax.ppermute(value, axis, pairs)]
    dot_general x60 -> x2, matrix products: 98.2 us -> 3.32 us  [dot_high(): return jnp.matmul(left_mat, right_mat, precision=PRECISE)]
    pallas_call x0 -> x5, Pallas kernels: none -> 70.7 us  [the longest x1 47 us: delta(): pl.pallas_call(functools.partial(relay_kernel, n), out_shape=(state, stat...]
    ppermute x28 -> x0, starting transfers between devices: 69.9 us -> none  [shifted(): return lax.ppermute(value, axis, pairs)]
    all_gather x0 -> x1, waiting for transfers between devices: none -> 49.3 us  [attention(): lax.all_gather(jnp.concatenate([attn_query, attn_key, attn_value, attn_ou...]
    dot_general x24 -> x1, matrix products: 49 us -> 0.64 us  [shards(): lax.dot_general(layer_input, both_weight, NT, preferred_element_type=F32)]
    reduce_scatter x2 -> x1, waiting for transfers between devices: 0.01 us -> 29.3 us  [shards(): lax.psum_scatter(terms, 'seq', scatter_dimension=1, tiled=True)]
  transfers between devices with their start and end apart: 32 -> 3, of which waited for: 19 -> 2; matrix products, arithmetic and copies ran while one was open for 4% -> 2% of each run, Pallas kernels for 0% -> 0%
where the time goes in v1:
time: 238 us
  waiting for transfers between devices  78.6 us (33%)
  Pallas kernels  70.7 us (30%)
  blocking collectives  55.3 us (23%)
  between operations  14.3 us (6%)
  local copies, waits for them, and re-layouts  9.55 us (4%)
  matrix products  3.96 us (2%)
  starting transfers between devices  3.5 us (1%)
    all_gather x1, waiting for transfers between devices, attention(): lax.all_gather(jnp.concatenate([attn_query, attn_key, attn_value, attn_ou...  49.3 us
    pallas_call x1, Pallas kernels, delta(): pl.pallas_call(functools.partial(relay_kernel, n), out_shape=(state, stat...  47 us
    all_gather x1, blocking collectives, attention(): every = lax.all_gather(stats, 'seq')  30.4 us
    reduce_scatter x1, waiting for transfers between devices, shards(): lax.psum_scatter(terms, 'seq', scatter_dimension=1, tiled=True)  29.3 us
    psum x1, blocking collectives, shards(): params = lax.psum(jnp.stack([grad_rate, grad_bias]), 'seq')  19.7 us
    pallas_call x1, Pallas kernels, delta(): pl.pallas_call(local_kernel, grid=(steps,), out_shape=(state, state, stat...  9.14 us
    pallas_call x1, Pallas kernels, delta(): pl.pallas_call(grads_kernel, grid=(steps,), out_shape=(flat, flat, flat,...  8.91 us
    all_gather x1, blocking collectives, shards(): every = lax.all_gather(mine, 'head', axis=1, tiled=True)  5.19 us
  transfers between devices with their start and end apart: 3, of which 2 were waited for; matrix products, arithmetic and copies ran while one was open for 2% of the time, Pallas kernels for 0%

profile of v1, /device:TPU:0, one launch (start us, length us, event | category | flops | bytes accessed | tf_op | source)
XLA Modules:
  0.0 237.7 jit_solution(3772152744340224778)
XLA Ops:
  7.2 0.0 copy-start
  7.2 0.0 copy-start.17
  7.2 0.0 copy-start.9
  7.2 0.0 copy-start.10
  7.2 0.0 copy-start.11
  7.2 0.0 copy-start.12
  7.2 0.0 reduce-scatter.2.cloned.1.call-start
  7.3 1.1 constant_dynamic-update-slice_fusion.1
  8.4 0.7 exponential_negate_fusion
  9.0 0.9 constant_dynamic-update-slice_fusion
  9.9 0.0 copy-done
  10.0 0.0 copy-start.15
  10.0 0.6 convolution_bitcast_fusion
  10.6 0.0 copy-done.17
  10.6 0.1 broadcast_multiply_fusion
  10.7 0.0 copy-done.15
  10.7 0.1 copy.36
  10.9 0.1 copy.37
  11.0 0.0 copy-done.9
  11.0 0.0 copy-done.10
  11.0 0.0 copy-done.11
  11.0 0.0 copy-done.12
  11.0 0.0 copy-start.3
  11.1 0.0 copy-start.4
  11.1 9.1 %delta_local.1 = (f32[8,128,128]{2,1,0:T(8,128)S(1)}, f32[8,128,128]{2,1,0:T(8,128)S(1)}, f32[8,128,128]{2,1,0:T(8,128)S(1)}, f32[8,128,128]{2,1,0:T(8,128)S(1)}...) custom-call(bf16[128,1024]{1,0:T(8,128)(2,1)S(1)} %copy-done.9, ...), custom_call_target="tpu_custom_call" | custom-call | flops 2013265920 | bytes 6291456 | tf_op jit(solution)/shard_map/delta_local/pallas_call | solution.py:367
  20.2 0.0 copy-start.14
  20.2 0.8 copy-done.14
  21.0 0.0 copy-done.3
  21.0 0.0 copy-done.4
  21.0 47.0 %state_relay.1 = (f32[8,128,128]{2,1,0:T(8,128)S(1)}, f32[8,128,128]{2,1,0:T(8,128)S(1)}) custom-call(f32[8,128,128]{2,1,0:T(8,128)S(1)} %get-tuple-element.32.transit_ref, f32[8,128,128]{2,1,0:T(8,128)S(1)} %get-tuple-element.33.offset_ref, f32[8,128,128]{2,1,0:T(8,128)S(1)} %get-tuple-element.34.lgrad_ref, f32[8,128,128]{2,1,0:T(8,128)S(1)} %copy-done.3, ...), custom_call_target="tpu_custom_call" | custom-call | flops 201326592 | bytes 4194304 | tf_op jit(solution)/shard_map/state_relay/pallas_call | solution.py:379
  68.1 0.0 copy-done.13
  68.1 8.9 %delta_grads.1 = (f32[128,1024]{1,0:T(8,128)}, f32[128,1024]{1,0:T(8,128)}, f32[128,1024]{1,0:T(8,128)}, f32[1,8,128,128]{3,2,1,0:T(8,128)}, f32[2,128,4]{2,1,0:T(8,128)S(1)}, /*index=5*/f32[2,128,4]{2,1,0:T(8,128)S(1)}) custom-call(bf16[128,1024]{1,0:T(8,128)(2,1)S(1)} %copy-done.9, bf16[128,1024]{1,0:T(8,128)(2,1)S(1)} %copy-done.10, ...), custom_call_target="tpu_custom_call" | custom-call | flops 1677721600 | bytes 9437184 | tf_op jit(solution)/shard_map/delta_grads/pallas_call | solution.py:392
  77.0 0.0 copy-start.7
  77.0 0.0 copy-start.8
  77.0 0.1 copy.38
  77.1 0.1 copy.39
  77.2 0.3 fusion.8
  77.4 0.0 copy-start.18
  77.4 1.7 fusion.7
  79.2 0.0 reduce-scatter.2.cloned.1.call-update
  79.2 0.0 all-gather.4.cloned.1.call-start
  79.2 0.0 copy-done.5
  79.3 0.0 copy-done.6
  79.3 0.0 copy-done.7
  79.3 0.0 copy-done.8
  79.3 0.7 pad_maximum_fusion
  80.0 0.0 all-gather.4.cloned.1.call-update
  80.1 0.7 copy.45
  80.8 3.4 %all-to-all-start = ((bf16[16,4,2048]{2,0,1:T(8,128)(2,1)}), bf16[16,4,2048]{2,0,1:T(8,128)(2,1)S(1)}, u32[]{:S(2)}, u32[]{:S(2)}) async-start(bf16[16,4,2048]{2,0,1:T(8,128)(2,1)} %bitcast.32), calls=%async_computation | async-start | bytes 524288 | tf_op jit(solution)/shard_map/all_to_all | solution.py:431
  84.2 19.7 %psum.7 = f32[2,8]{1,0:T(2,128)S(1)} all-reduce(f32[2,8]{1,0:T(2,128)S(1)} %pad_maximum_fusion.2), channel_id=1, replica_groups=mesh['seq'=8,'head'=4] {'seq'}, use_global_device_ids=true, to_apply=%region_3.4 | all-reduce | flops 16 | bytes 128 | tf_op jit(solution)/shard_map/psum | solution.py:442
  103.9 5.2 %all_gather.15 = f32[128,64]{0,1:T(8,128)S(1)} all-gather(f32[128,16]{0,1:T(8,128)S(1)} %pad_maximum_fusion.1), channel_id=1, replica_groups=mesh['seq'=8,'head'=4] {'head'}, dimensions={1}, use_global_device_ids=true | all-gather | bytes 40960 | tf_op jit(solution)/shard_map/all_gather | solution.py:438
  109.1 0.5 slice_bitcast_fusion
  109.6 0.0 all-to-all-done
  109.6 1.6 fusion.11
  111.2 29.3 %reduce-scatter.2.cloned.1.call-done = f32[16,1024]{1,0:T(8,128)} async-done(((f32[16,8192]{1,0:T(8,128)}), f32[16,1024]{1,0:T(8,128)}) %reduce-scatter.2.cloned.1.call-update) | async-done | bytes 65552 | tf_op jit(solution)/shard_map/reduce_scatter | solution.py:441
  140.5 1.4 fusion.10
  141.9 49.3 %all-gather.4.cloned.1.call-done = bf16[1024,1024]{1,0:T(8,128)(2,1)} async-done(((bf16[128,1024]{1,0:T(8,128)(2,1)}), bf16[1024,1024]{1,0:T(8,128)(2,1)}) %all-gather.4.cloned.1.call-update) | async-done | bytes 2097168 | tf_op jit(solution)/shard_map/all_gather | solution.py:303
  191.2 1.6 copy-done.1
  192.8 2.6 %attn_rows.1 = (f32[128,256]{1,0:T(8,128)}, f32[2,128,3]{2,1,0:T(8,128)S(1)}) custom-call(s32[1]{0:T(128)} %bitcast.15.start_ref, bf16[128,256]{1,0:T(8,128)(2,1)S(1)} %copy-done.5, bf16[128,256]{1,0:T(8,128)(2,1)S(1)} %copy-done.6, bf16[8,128,1024]{2,1,0:T(8,128)(2,1)S(1)} %bitcast.33, bf16[8,128,1024]{2,1,0:T(8,128)(2,1)S(1)} %bitcast.34), custom_call_target="tpu_custom_call" | custom-call | flops 201326592 | bytes 2097152 | tf_op jit(solution)/shard_map/attn_rows/pallas_call | solution.py:322
  195.4 0.1 copy.41
  195.5 30.4 %all-gather.1 = f32[16,128,3]{1,2,0:T(4,128)S(1)} all-gather(f32[2,128,3]{1,2,0:T(4,128)S(1)} %copy.41), channel_id=3, replica_groups=mesh['seq'=8,'head'=4] {'seq'}, dimensions={0}, use_global_device_ids=true | all-gather | bytes 27648 | tf_op jit(solution)/shard_map/all_gather | solution.py:330
  225.9 0.4 copy.42
  226.3 1.6 copy-done.2
  227.9 3.0 %attn_keys.1 = (f32[128,256]{1,0:T(8,128)}, f32[128,256]{1,0:T(8,128)}) custom-call(s32[1]{0:T(128)} %bitcast.17.start_ref, bf16[128,256]{1,0:T(8,128)(2,1)S(1)} %copy-done.8, bf16[128,256]{1,0:T(8,128)(2,1)S(1)} %copy-done.7, bf16[8,128,1024]{2,1,0:T(8,128)(2,1)S(1)} %bitcast.35, bf16[8,128,1024]{2,1,0:T(8,128)(2,1)S(1)} %bitcast.36, ...), custom_call_target="tpu_custom_call" | custom-call | flops 201326592 | bytes 2097152 | tf_op jit(solution)/shard_map/attn_keys/pallas_call | solution.py:333
  (11 shorter events, 0.0 us)
Async XLA Ops:
  7.2 2.8 %copy-start = (bf16[128,8192]{1,0:T(8,128)(2,1)S(1)}, bf16[128,8192]{1,0:T(8,128)(2,1)}, u32[]{:S(2)}) copy-start(bf16[128,8192]{1,0:T(8,128)(2,1)} %param.15) | copy-start | bytes 6291460
  7.2 3.4 %copy-start.17 = (f32[8]{0:T(128)S(1)}, f32[8]{0:T(128)}, u32[]{:S(2)}) copy-start(f32[8]{0:T(128)} %param.19) | copy-start | bytes 100
  7.2 3.8 %copy-start.9 = (bf16[128,1024]{1,0:T(8,128)(2,1)S(1)}, bf16[128,1024]{1,0:T(8,128)(2,1)}, u32[]{:S(2)}) copy-start(bf16[128,1024]{1,0:T(8,128)(2,1)} %q_ref.4) | copy-start | bytes 786436
  7.2 3.8 %copy-start.10 = (bf16[128,1024]{1,0:T(8,128)(2,1)S(1)}, bf16[128,1024]{1,0:T(8,128)(2,1)}, u32[]{:S(2)}) copy-start(bf16[128,1024]{1,0:T(8,128)(2,1)} %k_ref.4) | copy-start | bytes 786436
  7.2 3.8 %copy-start.11 = (bf16[128,1024]{1,0:T(8,128)(2,1)S(1)}, bf16[128,1024]{1,0:T(8,128)(2,1)}, u32[]{:S(2)}) copy-start(bf16[128,1024]{1,0:T(8,128)(2,1)} %v_ref.4) | copy-start | bytes 786436
  7.2 3.8 %copy-start.12 = (bf16[128,1024]{1,0:T(8,128)(2,1)S(1)}, bf16[128,1024]{1,0:T(8,128)(2,1)}, u32[]{:S(2)}) copy-start(bf16[128,1024]{1,0:T(8,128)(2,1)} %do_ref.3) | copy-start | bytes 786436
  7.2 133.3 %reduce-scatter.2.cloned.1.call-start = ((), (), s32[]{:S(2)}) async-start(), calls=%async_computation.2 | async-start | bytes 589824 | tf_op jit(solution)/shard_map/reduce_scatter | solution.py:441
  10.0 0.8 copy-start.15
  11.0 10.0 %copy-start.3 = (f32[8,128,128]{2,1,0:T(8,128)S(1)}, f32[8,128,128]{2,1,0:T(8,128)}, u32[]{:S(2)}) copy-start(f32[8,128,128]{2,1,0:T(8,128)} %init_ref.1) | copy-start | bytes 1572868
  11.1 10.0 %copy-start.4 = (f32[8,128,128]{2,1,0:T(8,128)S(1)}, f32[8,128,128]{2,1,0:T(8,128)}, u32[]{:S(2)}) copy-start(f32[8,128,128]{2,1,0:T(8,128)} %next_ref.1) | copy-start | bytes 1572868
  20.2 0.8 copy-start.14
  21.0 47.0 %copy-start.13 = (bf16[128,1024]{1,0:T(8,128)(2,1)S(1)}, bf16[128,1024]{1,0:T(8,128)(2,1)}, u32[]{:S(2)}) copy-start(bf16[128,1024]{1,0:T(8,128)(2,1)} %do_ref.3) | copy-start | bytes 786436
  77.0 2.3 copy-start.5
  77.0 2.3 copy-start.6
  77.0 2.3 copy-start.7
  77.0 2.3 copy-start.8
  77.0 3.0 %copy-start.16 = (bf16[16,8192]{1,0:T(8,128)(2,1)S(1)}, bf16[16,8192]{1,0:T(8,128)(2,1)}, u32[]{:S(2)}) copy-start(bf16[16,8192]{1,0:T(8,128)(2,1)} %copy-done.15) | copy-start | bytes 786436
  77.4 3.4 %copy-start.18 = (f32[8]{0:T(128)S(1)}, f32[8]{0:T(128)}, u32[]{:S(2)}) copy-start(f32[8]{0:T(128)} %param.18) | copy-start | bytes 100
  79.2 112.0 %all-gather.4.cloned.1.call-start = ((), (), s32[]{:S(2)}) async-start(), calls=%async_computation.3 | async-start | bytes 2359296 | tf_op jit(solution)/shard_map/all_gather | solution.py:303
  80.8 28.8 %all-to-all-start = ((bf16[16,4,2048]{2,0,1:T(8,128)(2,1)}), bf16[16,4,2048]{2,0,1:T(8,128)(2,1)S(1)}, u32[]{:S(2)}, u32[]{:S(2)}) async-start(bf16[16,4,2048]{2,0,1:T(8,128)(2,1)} %bitcast.32), calls=%async_computation | async-start | bytes 524288 | tf_op jit(solution)/shard_map/all_to_all | solution.py:431
  191.2 1.6 copy-start.1
  226.3 1.6 copy-start.2
Sparse Core Ops, SparseCore 0:
  79.3 61.1 reduce-scatter.1
  142.8 48.3 all-gather.3

commit v2 on v1

v2 whole, which is shorter than its diff:
```python
import functools
import math

import jax
import jax.numpy as jnp
from jax import lax
from jax.experimental import pallas as pl
from jax.experimental.pallas import tpu as pltpu
from jax.sharding import PartitionSpec as P

AHD = 128
WINDOW = 1024
HOP_TICKS = 3
MESH = pl.DeviceIdType.MESH
F32 = jnp.float32
BF16 = jnp.bfloat16
NN = (((1,), (0,)), ((), ()))
NT = (((1,), (1,)), ((), ()))
TN = (((0,), (0,)), ((), ()))


def parts(value):
    if isinstance(value, tuple):
        return value
    if value.dtype == BF16:
        return (value,)
    high = value.astype(BF16)
    return (high, (value - high.astype(F32)).astype(BF16))


def mul(left, right, dims=NN):
    left, right = parts(left), parts(right)
    total = None
    for i, a in reversed(list(enumerate(left))):
        for j, b in reversed(list(enumerate(right))):
            if i + j < 2:
                term = lax.dot_general(a, b, dims, preferred_element_type=F32)
                total = term if total is None else total + term
    return total


def row_sum(value):
    return jnp.sum(value, axis=1, keepdims=True)


def col_sum(value):
    return jnp.sum(value, axis=0, keepdims=True)


def grids(size):
    rows = lax.broadcasted_iota(jnp.int32, (size, size), 0)
    cols = lax.broadcasted_iota(jnp.int32, (size, size), 1)
    return rows, cols


def as_row(col, rows, cols):
    return col_sum(jnp.where(rows == cols, col, 0.0))


def as_col(row, rows, cols):
    return row_sum(jnp.where(rows == cols, row, 0.0))


def head_terms(q, k, decay_row, rows, cols):
    kf = k.astype(F32)
    qf = q.astype(F32)
    k_norm = lax.rsqrt(row_sum(kf * kf) + 1e-06)
    q_norm = lax.rsqrt(row_sum(qf * qf) + 1e-06)
    rk = k_norm
    rq = q_norm * (1.0 / math.sqrt(q.shape[1]))
    cum = row_sum(jnp.where(cols <= rows, decay_row, 0.0))
    cum_row = as_row(cum, rows, cols)
    lower = rows >= cols
    ratios = jnp.where(lower, jnp.exp(jnp.where(lower, cum - cum_row, 0.0)), 0.0)
    growth = jnp.exp(cum)
    last = row_sum(decay_row)
    tail = jnp.exp(last - cum)
    return kf, qf, k_norm, q_norm, rk, rq, ratios, growth, jnp.exp(last), tail


def local_kernel(q_ref, k_ref, v_ref, do_ref, beta_ref, decay_ref,
                 transit_ref, offset_ref, lgrad_ref, t_ref, w_ref, uv_ref, p_ref, n_ref):
    size = q_ref.shape[0]
    count = beta_ref.shape[1]
    width = q_ref.shape[1] // count
    rows, cols = grids(size)
    inverses, systems, kept = [], [], []
    for j in range(count):
        lanes = slice(j * width, (j + 1) * width)
        q, k = q_ref[:, lanes], k_ref[:, lanes]
        beta, decay = as_col(beta_ref[0, j:j + 1, :], rows, cols), decay_ref[0, j:j + 1, :]
        kf, qf, _, _, rk, rq, ratios, growth, last, tail = head_terms(q, k, decay, rows, cols)
        rk_row = as_row(rk, rows, cols)
        near = jnp.where(rows > cols, ratios * (mul(k, k, NT) * rk * rk_row), 0.0)
        mixing = ratios * (mul(q, k, NT) * rq * rk_row)
        n_ref[j] = near
        p_ref[j] = mixing
        systems.append(beta * near)
        kept.append((kf * rk, qf * rq, beta, growth, last, tail, mixing))
        pair = (rows // 2 == cols // 2) & (rows > cols)
        inverses.append(jnp.where(rows == cols, 1.0, jnp.where(pair, -systems[-1], 0.0)))
    span = 2
    while span < size:
        mask = (rows // (2 * span) == cols // (2 * span)) & (rows // span > cols // span)
        split = [parts(inverse) for inverse in inverses]
        halves = [mul(split[j], jnp.where(mask, systems[j], 0.0)) for j in range(count)]
        inverses = [inverses[j] - mul(halves[j], split[j]) for j in range(count)]
        span *= 2
    for j in range(count):
        lanes = slice(j * width, (j + 1) * width)
        keys, queries, beta, growth, last, tail, mixing = kept[j]
        t_ref[j] = inverses[j]
        split = parts(inverses[j])
        w_all = mul(split, (beta * growth) * keys)
        uv_all = mul(split, beta * v_ref[:, lanes].astype(F32))
        w_ref[j] = w_all
        uv_ref[j] = uv_all
        w_split = parts(w_all)
        tail_keys = parts(keys * tail)
        transit_ref[j] = jnp.where(rows == cols, last, 0.0) - mul(tail_keys, w_split, TN)
        offset_ref[j] = mul(tail_keys, uv_all, TN)
        reach = growth * queries - mul(mixing, w_split)
        lgrad_ref[j] = mul(reach, do_ref[:, lanes], TN)


def meet(n, m, me, head):
    barrier = pltpu.get_barrier_semaphore()
    for d in range(1, n):
        pl.semaphore_signal(barrier, inc=1, device_id=(lax.rem(me + d, n), head),
                            device_id_type=MESH)
    for d in range(1, m):
        pl.semaphore_signal(barrier, inc=1, device_id=(me, lax.rem(head + d, m)),
                            device_id_type=MESH)
    return lambda: pl.semaphore_wait(barrier, n + m - 2)


def remote(src, dst, send, recv, device):
    return pltpu.make_async_remote_copy(src_ref=src, dst_ref=dst, send_sem=send, recv_sem=recv,
                                        device_id=device, device_id_type=MESH)


def relay_kernel(n, m, span, q_ref, k_ref, v_ref, do_ref, beta_ref, decay_ref, init_ref, next_ref,
                 bw_ref, dw_ref, aq_ref, ak_ref, av_ref, ag_ref,
                 transit_ref, lgrad_ref, t_ref, w_ref, uv_ref, p_ref, n_ref, mem_ref, grad_ref,
                 weight_ref, kv_ref, qg_ref,
                 offset_ref, slices, send_f, recv_f, send_b, recv_b, sf_sem, rf_sem, sb_sem, rb_sem,
                 skv_sem, rkv_sem, sqg_sem, rqg_sem, sw_sem, rw_sem):
    me = lax.axis_index("seq")
    head = lax.axis_index("head")
    heads = init_ref.shape[0]
    steps, group, _ = beta_ref.shape
    right, left = lax.rem(me + 1, n), lax.rem(me + n - 1, n)
    has_left, has_right = me > 0, me < n - 1
    entered = meet(n, m, me, head)
    width = ak_ref.shape[1]
    kv_ref[0, :, :width] = ak_ref[...]
    kv_ref[0, :, width:] = av_ref[...]
    qg_ref[0, :, :width] = aq_ref[...]
    qg_ref[0, :, width:] = ag_ref[...]
    part = bw_ref.shape[1] // m
    for p in range(m):
        lanes = slice(p * part, (p + 1) * part)
        slices[p, :heads] = bw_ref[:, lanes].astype(F32)
        slices[p, heads:] = dw_ref[:, lanes].astype(F32)
    weight_ref[head] = slices[head]
    entered()

    def copy_kv(d):
        return remote(kv_ref.at[0], kv_ref.at[d], skv_sem.at[d], rkv_sem.at[d],
                      (lax.rem(me + d, n), head))

    def copy_qg(d):
        return remote(qg_ref.at[0], qg_ref.at[d], sqg_sem.at[d], rqg_sem.at[d],
                      (lax.rem(me + n - d, n), head))

    def copy_weight(d):
        peer = lax.rem(head + d, m)
        return remote(slices.at[peer], weight_ref.at[head], sw_sem.at[d], rw_sem.at[d], (me, peer))

    def came_weight(d):
        peer = lax.rem(head + m - d, m)
        return remote(slices.at[peer], weight_ref.at[peer], sw_sem.at[d], rw_sem.at[d], (me, peer))

    for d in range(1, m):
        copy_weight(d).start()
    for d in range(1, span):
        @pl.when(me + d < n)
        def _(d=d):
            copy_kv(d).start()

        @pl.when(me >= d)
        def _(d=d):
            copy_qg(d).start()

        @pl.when(me < d)
        def _(d=d):
            kv_ref[d] = jnp.zeros(kv_ref.shape[1:], BF16)

        @pl.when(me + d >= n)
        def _(d=d):
            qg_ref[d] = jnp.zeros(qg_ref.shape[1:], BF16)

    lane_count = q_ref.shape[1] // steps

    def local_step(i, carry):
        lanes = pl.ds(pl.multiple_of(i * lane_count, 128), lane_count)
        mine = pl.ds(i * group, group)
        local_kernel(q_ref.at[:, lanes], k_ref.at[:, lanes], v_ref.at[:, lanes],
                     do_ref.at[:, lanes], beta_ref.at[pl.ds(i, 1)], decay_ref.at[pl.ds(i, 1)],
                     transit_ref.at[mine], offset_ref.at[mine], lgrad_ref.at[mine], t_ref.at[mine],
                     w_ref.at[mine], uv_ref.at[mine], p_ref.at[mine], n_ref.at[mine])
        return carry

    lax.fori_loop(0, steps, local_step, 0)

    def copy_f(h):
        return pltpu.make_async_remote_copy(
            src_ref=send_f.at[h], dst_ref=recv_f.at[h], send_sem=sf_sem.at[h],
            recv_sem=rf_sem.at[h], device_id=(right, head), device_id_type=MESH)

    def copy_b(h):
        return pltpu.make_async_remote_copy(
            src_ref=send_b.at[h], dst_ref=recv_b.at[h], send_sem=sb_sem.at[h],
            recv_sem=rb_sem.at[h], device_id=(left, head), device_id_type=MESH)

    def tick(t, carry):
        hf = t - HOP_TICKS * me
        hb = t - HOP_TICKS * (n - 1 - me)

        @pl.when((hf >= 0) & (hf < heads))
        def _():
            @pl.when(has_left)
            def _():
                copy_f(hf).wait_recv()
                mem_ref[hf] = recv_f[hf]

            @pl.when(jnp.logical_not(has_left))
            def _():
                mem_ref[hf] = init_ref[hf]

            @pl.when(has_right)
            def _():
                send_f[hf] = mul(transit_ref[hf], mem_ref[hf]) + offset_ref[hf]
                copy_f(hf).start()

        @pl.when((hb >= 0) & (hb < heads))
        def _():
            @pl.when(has_right)
            def _():
                copy_b(hb).wait_recv()
                grad_ref[hb] = recv_b[hb]

            @pl.when(jnp.logical_not(has_right))
            def _():
                grad_ref[hb] = next_ref[hb]

            @pl.when(has_left)
            def _():
                send_b[hb] = mul(transit_ref[hb], grad_ref[hb], TN) + lgrad_ref[hb]
                copy_b(hb).start()

        return carry

    lax.fori_loop(0, HOP_TICKS * (n - 1) + heads, tick, 0)

    def drain(h, carry):
        @pl.when(has_right)
        def _():
            copy_f(h).wait_send()

        @pl.when(has_left)
        def _():
            copy_b(h).wait_send()

        return carry

    lax.fori_loop(0, heads, drain, 0)
    for d in range(1, m):
        came_weight(d).wait_recv()
        copy_weight(d).wait_send()
    for d in range(1, span):
        @pl.when(me + d < n)
        def _(d=d):
            copy_kv(d).wait_send()
            copy_qg(d).wait_recv()

        @pl.when(me >= d)
        def _(d=d):
            copy_qg(d).wait_send()
            copy_kv(d).wait_recv()


def grads_kernel(q_ref, k_ref, v_ref, do_ref, beta_ref, decay_ref, mem_ref, grad_ref,
                 transit_ref, lgrad_ref, t_ref, w_ref, uv_ref, p_ref, n_ref,
                 dq_ref, dk_ref, dv_ref, bound_ref, dbeta_ref, ddecay_ref):
    size = q_ref.shape[0]
    count = beta_ref.shape[1]
    width = q_ref.shape[1] // count
    rows, cols = grids(size)
    for j in range(count):
        lanes = slice(j * width, (j + 1) * width)
        q, k, do = q_ref[:, lanes], k_ref[:, lanes], do_ref[:, lanes]
        beta, decay = as_col(beta_ref[0, j:j + 1, :], rows, cols), decay_ref[0, j:j + 1, :]
        kf, qf, k_norm, q_norm, rk, rq, ratios, growth, last, tail = head_terms(
            q, k, decay, rows, cols)
        rk_row = as_row(rk, rows, cols)
        dof = do.astype(F32)
        memory, grad = mem_ref[j], grad_ref[j]
        near, mixing = n_ref[j], p_ref[j]
        mem_s, grad_s = parts(memory), parts(grad)
        updates = uv_ref[j] - mul(w_ref[j], mem_s)
        up_s = parts(updates)
        q_mem = rq * mul(q, mem_s)
        k_mem = rk * mul(k, mem_s)
        dup = mul(mixing, do, TN) + (rk * tail) * mul(k, grad_s)
        drhs = mul(t_ref[j], dup, TN)
        drhs_s = parts(drhs)
        dmix = jnp.where(rows >= cols, mul(do, up_s, NT), 0.0)
        dqk = dmix * ratios
        dsys = jnp.where(rows > cols, -mul(drhs_s, up_s, NT), 0.0)
        dgram = dsys * beta * ratios
        dval = beta * drhs
        dquery = growth * mul(do, mem_s, NT) + mul(dqk * rk_row, k)
        dtail = mul(up_s, grad_s, NT)
        dkey = mul(dqk * rq, q, TN) + dtail * tail
        dkey = dkey - (beta * growth) * mul(drhs_s, mem_s, NT)
        dkey = dkey + mul((dgram + dgram.T) * rk_row, k)
        dbeta = row_sum(drhs * (v_ref[:, lanes].astype(F32) - growth * k_mem))
        dbeta_ref[0, j:j + 1, :] = as_row(dbeta + row_sum(dsys * near), rows, cols)
        inner = dsys * (beta * near) + dmix * mixing
        tails = row_sum(dtail * kf) * (rk * tail)
        dcum = growth * (row_sum(dof * q_mem) - row_sum(dval * k_mem)) - tails + row_sum(inner)
        dcum_row = as_row(dcum, rows, cols) - col_sum(inner)
        at_end = col_sum(tails) + last * col_sum(row_sum(grad * memory))
        after = row_sum(jnp.where(cols >= rows, dcum_row, 0.0)) + at_end
        ddecay_ref[0, j:j + 1, :] = as_row(after, rows, cols)
        dq_ref[:, lanes] = rq * (dquery - qf * (q_norm * q_norm * row_sum(qf * dquery)))
        dk_ref[:, lanes] = rk * (dkey - kf * (k_norm * k_norm * row_sum(kf * dkey)))
        dv_ref[:, lanes] = dval
        bound_ref[0, j] = mul(transit_ref[j], grad_s, TN) + lgrad_ref[j]


def attn_rows_kernel(place_ref, q_ref, g_ref, k_ref, v_ref, dq_ref, stat_ref):
    size = q_ref.shape[0]
    count = k_ref.shape[0]
    span = count * size
    scale = 1.0 / math.sqrt(AHD)
    keys = k_ref[...].reshape(span, AHD)
    values = v_ref[...].reshape(span, AHD)
    rows = lax.broadcasted_iota(jnp.int32, (size, span), 0)
    cols = lax.broadcasted_iota(jnp.int32, (size, span), 1)
    back = cols // size
    gap = rows - cols % size + back * size
    allowed = (gap >= 0) & (gap < WINDOW) & (back <= place_ref[0])
    scores = jnp.where(allowed, mul(q_ref[...], keys, NT) * scale, -1e30)
    top = jnp.max(scores, axis=1, keepdims=True)
    weights = jnp.exp(scores - top)
    inverse = 1.0 / row_sum(weights)
    weights = weights * inverse
    weight_grad = mul(g_ref[...], values, NT)
    row_term = row_sum(weights * weight_grad)
    dscores = weights * (weight_grad - row_term) * scale
    dq_ref[...] = mul(dscores, keys)
    square = grids(size)
    stat_ref[0] = jnp.zeros(stat_ref.shape[1:], F32)
    stat_ref[0, 0:1, :] = as_row(top, *square)
    stat_ref[0, 1:2, :] = as_row(inverse, *square)
    stat_ref[0, 2:3, :] = as_row(row_term, *square)


def tail_kernel(n, m, span, x_ref, dbeta_ref, ddecay_ref, beta_ref, decay_ref, slope_ref,
                weight_ref, ak_ref, av_ref, qg_ref, stat_ref,
                input_ref, wsum_ref, dk_ref, dv_ref,
                terms, arrived, every, stats, st_sem, rt_sem, se_sem, re_sem, ss_sem, rs_sem):
    me = lax.axis_index("seq")
    head = lax.axis_index("head")
    entered = meet(n, m, me, head)
    heads, size = beta_ref.shape
    part = x_ref.shape[1] // n
    betas, ddecay = beta_ref[...], ddecay_ref[...]
    grad_d = ddecay * slope_ref[...]
    every[head, :heads] = dbeta_ref[...] * (betas * (1.0 - betas))
    every[head, heads:] = grad_d
    stats[0] = stat_ref[...]
    lane = lax.broadcasted_iota(jnp.int32, (heads, size), 1)
    params = jnp.where(lane == 0, row_sum(ddecay * decay_ref[...]),
                       jnp.where(lane == 1, row_sum(grad_d), 0.0))
    mine = parts(every[head])
    entered()

    def copy_stat(d):
        return remote(stats.at[0], stats.at[d], ss_sem.at[d], rs_sem.at[d],
                      (lax.rem(me + n - d, n), head))

    def copy_every(d):
        return remote(every.at[head], every.at[head], se_sem.at[d], re_sem.at[d],
                      (me, lax.rem(head + d, m)))

    def came_every(d):
        peer = lax.rem(head + m - d, m)
        return remote(every.at[peer], every.at[peer], se_sem.at[d], re_sem.at[d], (me, peer))

    def copy_term(d):
        return remote(terms.at[d], arrived.at[d], st_sem.at[d], rt_sem.at[d],
                      (lax.rem(me + d, n), head))

    for d in range(1, span):
        @pl.when(me >= d)
        def _(d=d):
            copy_stat(d).start()

        @pl.when(me + d >= n)
        def _(d=d):
            stats[d] = jnp.zeros(stats.shape[1:], F32)
    for d in range(1, m):
        copy_every(d).start()

    def fill(d):
        place = pl.multiple_of(lax.rem(me + d, n) * part, 128)
        terms[d] = jnp.zeros(terms.shape[1:], F32)
        terms[d, :2 * heads] = mul(mine, x_ref[:, pl.ds(place, part)])
        terms[d, 2 * heads:, :size] = params

    def send_term(d, carry):
        fill(d)
        copy_term(d).start()
        return carry

    lax.fori_loop(1, n, send_term, 0)
    fill(0)
    for d in range(1, span):
        @pl.when(me + d < n)
        def _(d=d):
            copy_stat(d).wait_recv()
    scale = 1.0 / math.sqrt(AHD)
    rows, cols = grids(size)
    width = ak_ref.shape[1]
    for h in range(width // AHD):
        lanes = slice(h * AHD, (h + 1) * AHD)
        more = slice(width + h * AHD, width + (h + 1) * AHD)
        key, value = ak_ref[:, lanes], av_ref[:, lanes]
        dkey = dvalue = jnp.zeros((size, AHD), F32)
        for d in range(span):
            query, grad = qg_ref[d, :, lanes], qg_ref[d, :, more]
            gap = cols - rows + d * size
            allowed = (gap >= 0) & (gap < WINDOW)
            scores = mul(key, query, NT) * scale - stats[d, h, 0:1, :]
            weights = jnp.where(allowed, jnp.exp(jnp.where(allowed, scores, 0.0)), 0.0)
            weights = weights * stats[d, h, 1:2, :]
            dscores = weights * (mul(value, grad, NT) - stats[d, h, 2:3, :]) * scale
            dvalue = dvalue + mul(weights, grad)
            dkey = dkey + mul(dscores, query)
        dk_ref[:, lanes] = dkey
        dv_ref[:, lanes] = dvalue
    for d in range(1, m):
        came_every(d).wait_recv()
    left = parts(every[...].reshape(m * 2 * heads, size))
    chunk = next(c for c in (512, 256, 128) if weight_ref.shape[2] % c == 0)
    for c in range(0, weight_ref.shape[2], chunk):
        right = weight_ref[:, :, c:c + chunk].reshape(m * 2 * heads, chunk).astype(BF16)
        input_ref[:, c:c + chunk] = mul(left, right, TN)
    total = terms[0]
    for d in range(1, n):
        copy_term(d).wait_recv()
        total = total + arrived[d]
    wsum_ref[...] = total
    for d in range(1, span):
        @pl.when(me >= d)
        def _(d=d):
            copy_stat(d).wait_send()
    for d in range(1, m):
        copy_every(d).wait_send()
    for d in range(1, n):
        copy_term(d).wait_send()


def shards(layer_input, beta_weight, decay_weight, log_rate, decay_bias, delta_query, delta_key,
           delta_value, delta_out_grad, state_init, state_grad_next, attn_query, attn_key,
           attn_value, attn_out_grad):
    n, m = lax.axis_size("seq"), lax.axis_size("head")
    me = lax.axis_index("seq")
    size, width = delta_query.shape
    heads = beta_weight.shape[0]
    features = layer_input.shape[1]
    dim = width // heads
    group = next(c for c in (4, 2, 1) if heads % c == 0)
    steps = heads // group
    attn_width = attn_query.shape[1]
    attn_heads = attn_width // AHD
    span = min(-(-WINDOW // size), n - 1) + 1

    betas = jax.nn.sigmoid(lax.dot_general(beta_weight, layer_input, NT, preferred_element_type=F32))
    shifted = lax.dot_general(decay_weight, layer_input, NT, preferred_element_type=F32)
    shifted = shifted + decay_bias[:, None]
    rate = -jnp.exp(log_rate)[:, None]
    decays = rate * jax.nn.softplus(shifted)
    slope = rate * jax.nn.sigmoid(shifted)

    def shape(*dims, kind=F32):
        return jax.ShapeDtypeStruct(dims, kind)

    def params(mib, **more):
        return pltpu.CompilerParams(vmem_limit_bytes=mib * 1024 * 1024, **more)

    def cost(flops, mib):
        return pl.CostEstimate(flops=flops, bytes_accessed=mib << 20, transcendentals=0)

    vmem = pl.BlockSpec(memory_space=pltpu.VMEM)
    state, pair = shape(heads, dim, dim), shape(heads, size, size)
    per_token = shape(heads, size, dim)
    box, sem = pltpu.VMEM((heads, dim, dim), F32), pltpu.SemaphoreType.DMA
    beta_steps = betas.reshape(steps, group, size)
    decay_steps = decays.reshape(steps, group, size)
    flops = 2 * heads * size * size * dim
    (transit, lgrad, inverse, w_all, uv_all, mixing, near, mem_in, grad_end, weight_cols, kv_all,
     qg_all) = pl.pallas_call(
        functools.partial(relay_kernel, n, m, span),
        out_shape=(state, state, pair, per_token, per_token, pair, pair, state, state,
                   shape(m, 2 * heads, features // m),
                   shape(span, size, 2 * attn_width, kind=BF16),
                   shape(span, size, 2 * attn_width, kind=BF16)),
        in_specs=[vmem] * 14,
        out_specs=(vmem,) * 12,
        scratch_shapes=[box, pltpu.VMEM((m, 2 * heads, features // m), F32), box, box, box, box,
                        sem((heads,)), sem((heads,)), sem((heads,)), sem((heads,)),
                        sem((span,)), sem((span,)), sem((span,)), sem((span,)), sem((m,)), sem((m,))],
        compiler_params=params(48, collective_id=0, has_side_effects=True),
        name="state_relay", cost_estimate=cost(66 * flops, 16),
    )(delta_query, delta_key, delta_value, delta_out_grad, beta_steps, decay_steps, state_init,
      state_grad_next, beta_weight, decay_weight, attn_query, attn_key, attn_value, attn_out_grad)

    def own():
        return pl.BlockSpec((size, AHD), lambda h: (0, h))

    def others(part):
        return pl.BlockSpec((span, size, AHD), lambda h: (0, 0, part * attn_heads + h))

    attn_flops = 2 * size * span * size * attn_width
    dquery, stats = pl.pallas_call(
        attn_rows_kernel,
        grid=(attn_heads,),
        out_shape=(shape(size, attn_width), shape(attn_heads, 8, size)),
        in_specs=[pl.BlockSpec(memory_space=pltpu.SMEM), own(), own(), others(0), others(1)],
        out_specs=(own(), pl.BlockSpec((1, 8, size), lambda h: (h, 0, 0))),
        compiler_params=params(40), cost_estimate=cost(4 * attn_flops, 3), name="attn_rows",
    )(me.reshape(1).astype(jnp.int32), attn_query, attn_out_grad, kv_all, kv_all)

    tokens = pl.BlockSpec((size, group * dim), lambda i: (0, i))
    gate = pl.BlockSpec((1, group, size), lambda i: (i, 0, 0))
    square = pl.BlockSpec((group, dim, dim), lambda i: (i, 0, 0))
    pairs = pl.BlockSpec((group, size, size), lambda i: (i, 0, 0))
    token_rows = pl.BlockSpec((group, size, dim), lambda i: (i, 0, 0))
    flat, gate_out = shape(size, width), shape(steps, group, size)
    dq, dk, dv, boundary, dbeta, ddecay = pl.pallas_call(
        grads_kernel,
        grid=(steps,),
        out_shape=(flat, flat, flat, shape(1, heads, dim, dim), gate_out, gate_out),
        in_specs=[tokens] * 4 + [gate] * 2 + [square] * 4 + [pairs, token_rows, token_rows, pairs, pairs],
        out_specs=(tokens, tokens, tokens,
                   pl.BlockSpec((1, group, dim, dim), lambda i: (0, i, 0, 0)), gate, gate),
        compiler_params=params(48), name="delta_grads", cost_estimate=cost(50 * flops, 9),
    )(delta_query, delta_key, delta_value, delta_out_grad, beta_steps, decay_steps,
      mem_in, grad_end, transit, lgrad, inverse, w_all, uv_all, mixing, near)

    slot = pltpu.VMEM((n, 3 * heads, features // n), F32)
    input_grad, sums, dkey, dvalue = pl.pallas_call(
        functools.partial(tail_kernel, n, m, span),
        out_shape=(shape(size, features // m), shape(3 * heads, features // n),
                   shape(size, attn_width), shape(size, attn_width)),
        in_specs=[vmem] * 11,
        out_specs=(vmem,) * 4,
        scratch_shapes=[slot, slot, pltpu.VMEM((m, 2 * heads, size), F32),
                        pltpu.VMEM((span, attn_heads, 8, size), F32),
                        sem((n,)), sem((n,)), sem((m,)), sem((m,)), sem((span,)), sem((span,))],
        compiler_params=params(48, collective_id=1, has_side_effects=True),
        name="tail_exchange", cost_estimate=cost(4 * attn_flops, 6),
    )(layer_input, dbeta.reshape(heads, size), ddecay.reshape(heads, size), betas, decays, slope,
      weight_cols, attn_key, attn_value, qg_all, stats)
    return (dq, dk, dv, boundary, input_grad, sums[:heads], sums[heads:2 * heads],
            sums[2 * heads:, 0], sums[2 * heads:, 1], dquery, dkey, dvalue)


def solution(mesh):
    rows, heads, both = P("seq", None), P("head"), P("seq", "head")
    wide, state = P("head", None), P("head", None, None)
    return jax.shard_map(
        shards,
        mesh=mesh,
        in_specs=(rows, wide, wide, heads, heads, both, both, both, both, state, state,
                  both, both, both, both),
        out_specs=(both, both, both, P("seq", "head", None, None), both, P("head", "seq"),
                   P("head", "seq"), heads, heads, both, both, both),
        check_vma=False,
    )
```

time: 238 us -> 105 us (0.44)
  waiting for transfers between devices: 78.6 us -> 0 us
  blocking collectives: 55.3 us -> 0 us
  Pallas kernels: 70.7 us -> 95.3 us
  between operations: 14.3 us -> 0.84 us
  local copies, waits for them, and re-layouts: 9.55 us -> 4.72 us
  starting transfers between devices: 3.5 us -> 0 us
    all_gather x1 -> x0, waiting for transfers between devices: 49.3 us -> none  [attention(): lax.all_gather(jnp.concatenate([attn_query, attn_key, attn_value, attn_ou...]
    all_gather x2 -> x0, blocking collectives: 35.6 us -> none  [the longest x1 30.4 us: attention(): every = lax.all_gather(stats, 'seq')]
    reduce_scatter x1 -> x0, waiting for transfers between devices: 29.3 us -> none  [shards(): lax.psum_scatter(terms, 'seq', scatter_dimension=1, tiled=True)]
    pallas_call x5 -> x4, Pallas kernels: 70.7 us -> 95.3 us  [the longest x1 67 us: shards(): pl.pallas_call(functools.partial(relay_kernel, n, m, span), out_shape=(st...]
    psum x1 -> x0, blocking collectives: 19.7 us -> none  [shards(): params = lax.psum(jnp.stack([grad_rate, grad_bias]), 'seq')]
    all_to_all x1 -> x0, starting transfers between devices: 3.42 us -> none  [shards(): lax.all_to_all(both_weight, 'head', split_axis=1, concat_axis=0, tiled=True)]
    unnamed x39 -> x33, local copies, waits for them, and re-layouts: 5.12 us -> 3.4 us
  transfers between devices with their start and end apart: 3 -> 0, of which waited for: 2 -> 0; matrix products, arithmetic and copies ran while one was open for 2% -> 0% of each run, Pallas kernels for 0% -> 0%
where the time goes in v2:
time: 105 us
  Pallas kernels  95.3 us (91%)
  local copies, waits for them, and re-layouts  4.72 us (4%)
  matrix products  3 us (3%)
    pallas_call x1, Pallas kernels, shards(): pl.pallas_call(functools.partial(relay_kernel, n, m, span), out_shape=(st...  67 us
    pallas_call x1, Pallas kernels, shards(): pl.pallas_call(functools.partial(tail_kernel, n, m, span), out_shape=(sha...  17.9 us
    pallas_call x1, Pallas kernels, shards(): pl.pallas_call(grads_kernel, grid=(steps,), out_shape=(flat, flat, flat,...  7.83 us
    unnamed x33, local copies, waits for them, and re-layouts  3.4 us
    pallas_call x1, Pallas kernels, shards(): pl.pallas_call(attn_rows_kernel, grid=(attn_heads,), out_shape=(shape(siz...  2.6 us
    dot_general x1, matrix products, shards(): lax.dot_general(decay_weight, layer_input, NT, preferred_element_type=F32)  2.35 us

profile of v2, /device:TPU:0, one launch (start us, length us, event | category | flops | bytes accessed | tf_op | source)
XLA Modules:
  0.0 104.7 jit_solution(18410230479755523812)
XLA Ops:
  0.6 0.0 copy-start
  0.7 0.0 copy-start.4
  0.7 0.8 exponential_negate_fusion
  1.5 0.0 copy-start.5
  1.5 0.0 copy-start.6
  1.5 0.0 copy-start.7
  1.5 0.0 copy-start.8
  1.5 0.0 copy-start.9
  1.5 0.0 copy-start.10
  1.5 0.0 copy-start.11
  1.5 0.0 copy-start.12
  1.5 0.0 copy-start.13
  1.6 2.4 %divide_multiply_fusion = (f32[8,128]{1,0:T(8,128)S(1)}, f32[8,128]{1,0:T(8,128)S(1)}) fusion(f32[8]{0:T(128)S(1)} %exponential_negate_fusion, f32[8]{0:T(128)} %param.19, bf16[8,8192]{1,0:T(8,128)(2,1)} %dw_ref.1, bf16[128,8192]{1,0:T(8,128)(2,1)} %x_ref.1), kind=kOutput, calls=%fused_computation.9 | convolution fusion | flops 16789504 | bytes 2236480 | tf_op jit(solution)/shard_map/dot_general | solution.py:493
  3.9 0.0 copy-done
  3.9 0.0 copy-done.4
  3.9 0.6 fusion.2.beta_ref
  4.6 0.0 copy-done.5
  4.6 0.0 copy-done.6
  4.6 0.0 copy-done.7
  4.6 0.0 copy-done.8
  4.6 0.0 copy-done.9
  4.6 0.0 copy-done.10
  4.6 0.0 copy-done.11
  4.7 0.0 copy-done.12
  4.7 0.0 copy-done.13
  4.7 67.0 %state_relay.1 = (f32[8,128,128]{2,1,0:T(8,128)S(1)}, f32[8,128,128]{2,1,0:T(8,128)S(1)}, f32[8,128,128]{2,1,0:T(8,128)S(1)}, f32[8,128,128]{2,1,0:T(8,128)S(1)}...) custom-call(bf16[128,1024]{1,0:T(8,128)(2,1)S(1)} %copy-done.10, ...), custom_call_target="tpu_custom_call" | custom-call | flops 2214592512 | bytes 16777216 | tf_op jit(solution)/shard_map/state_relay/pallas_call | solution.py:516
  71.7 0.0 copy-start.14
  71.7 1.0 copy-done.14
  72.7 0.0 copy-start.1
  72.7 7.8 %delta_grads.1 = (f32[128,1024]{1,0:T(8,128)}, f32[128,1024]{1,0:T(8,128)}, f32[128,1024]{1,0:T(8,128)}, f32[1,8,128,128]{3,2,1,0:T(8,128)}, f32[2,4,128]{2,1,0:T(4,128)S(1)}, /*index=5*/f32[2,4,128]{2,1,0:T(4,128)S(1)}) custom-call(bf16[128,1024]{1,0:T(8,128)(2,1)S(1)} %copy-done.10, bf16[128,1024]{1,0:T(8,128)(2,1)S(1)} %copy-done.11, ...), custom_call_target="tpu_custom_call" | custom-call | flops 1677721600 | bytes 9437184 | tf_op jit(solution)/shard_map/delta_grads/pallas_call | solution.py:554
  80.5 0.0 copy-start.2
  80.5 0.0 copy-start.3
  80.5 0.0 copy-done.1
  80.6 2.6 %attn_rows.1 = (f32[128,256]{1,0:T(8,128)}, f32[2,8,128]{2,1,0:T(8,128)S(1)}) custom-call(s32[1]{0:T(128)} %bitcast.4.place_ref, bf16[128,256]{1,0:T(8,128)(2,1)S(1)} %copy-done.8, bf16[128,256]{1,0:T(8,128)(2,1)S(1)} %copy-done.9, bf16[8,128,512]{2,1,0:T(8,128)(2,1)S(1)} %copy-done.1, bf16[8,128,512]{2,1,0:T(8,128)(2,1)S(1)} %copy-done.1), custom_call_target="tpu_custom_call" | custom-call | flops 268435456 | bytes 3145728 | tf_op jit(solution)/shard_map/attn_rows/pallas_call | solution.py:539
  83.2 0.0 copy-done.2
  83.2 0.0 copy-done.3
  83.2 17.9 %tail_exchange.1 = (f32[128,2048]{1,0:T(8,128)S(1)}, f32[24,1024]{1,0:T(8,128)S(1)}, f32[128,256]{1,0:T(8,128)S(1)}, f32[128,256]{1,0:T(8,128)S(1)}) custom-call(bf16[128,8192]{1,0:T(8,128)(2,1)S(1)} %copy-done, f32[8,128]{1,0:T(8,128)S(1)} %bitcast.13, f32[8,128]{1,0:T(8,128)S(1)} %bitcast.14, f32[8,128]{1,0:T(8,128)S(1)} %fusion.2.beta_ref, ...), custom_call_target="tpu_custom_call" | custom-call | flops 268435456 | bytes 6291456 | tf_op jit(solution)/shard_map/tail_exchange/pallas_call | solution.py:566
  101.1 0.6 fusion.4
  101.7 0.7 slice_reduce_fusion
  102.4 1.0 copy.30
  103.4 0.7 copy.31
  104.0 0.7 copy.32
Async XLA Ops:
  0.6 3.3 %copy-start = (bf16[128,8192]{1,0:T(8,128)(2,1)S(1)}, bf16[128,8192]{1,0:T(8,128)(2,1)}, u32[]{:S(2)}) copy-start(bf16[128,8192]{1,0:T(8,128)(2,1)} %x_ref.1) | copy-start | bytes 6291460
  0.7 3.3 %copy-start.4 = (bf16[8,8192]{1,0:T(8,128)(2,1)S(1)}, bf16[8,8192]{1,0:T(8,128)(2,1)}, u32[]{:S(2)}) copy-start(bf16[8,8192]{1,0:T(8,128)(2,1)} %bw_ref.1) | copy-start | bytes 393220
  1.5 3.1 %copy-start.5 = (bf16[8,8192]{1,0:T(8,128)(2,1)S(1)}, bf16[8,8192]{1,0:T(8,128)(2,1)}, u32[]{:S(2)}) copy-start(bf16[8,8192]{1,0:T(8,128)(2,1)} %dw_ref.1) | copy-start | bytes 393220
  1.5 3.1 %copy-start.6 = (bf16[128,256]{1,0:T(8,128)(2,1)S(1)}, bf16[128,256]{1,0:T(8,128)(2,1)}, u32[]{:S(2)}) copy-start(bf16[128,256]{1,0:T(8,128)(2,1)} %ak_ref.3) | copy-start | bytes 196612
  1.5 3.1 %copy-start.7 = (bf16[128,256]{1,0:T(8,128)(2,1)S(1)}, bf16[128,256]{1,0:T(8,128)(2,1)}, u32[]{:S(2)}) copy-start(bf16[128,256]{1,0:T(8,128)(2,1)} %av_ref.3) | copy-start | bytes 196612
  1.5 3.1 %copy-start.8 = (bf16[128,256]{1,0:T(8,128)(2,1)S(1)}, bf16[128,256]{1,0:T(8,128)(2,1)}, u32[]{:S(2)}) copy-start(bf16[128,256]{1,0:T(8,128)(2,1)} %q_ref.5) | copy-start | bytes 196612
  1.5 3.1 %copy-start.9 = (bf16[128,256]{1,0:T(8,128)(2,1)S(1)}, bf16[128,256]{1,0:T(8,128)(2,1)}, u32[]{:S(2)}) copy-start(bf16[128,256]{1,0:T(8,128)(2,1)} %g_ref.1) | copy-start | bytes 196612
  1.5 3.1 %copy-start.10 = (bf16[128,1024]{1,0:T(8,128)(2,1)S(1)}, bf16[128,1024]{1,0:T(8,128)(2,1)}, u32[]{:S(2)}) copy-start(bf16[128,1024]{1,0:T(8,128)(2,1)} %q_ref.4) | copy-start | bytes 786436
  1.5 3.1 %copy-start.11 = (bf16[128,1024]{1,0:T(8,128)(2,1)S(1)}, bf16[128,1024]{1,0:T(8,128)(2,1)}, u32[]{:S(2)}) copy-start(bf16[128,1024]{1,0:T(8,128)(2,1)} %k_ref.3) | copy-start | bytes 786436
  1.5 3.1 %copy-start.12 = (bf16[128,1024]{1,0:T(8,128)(2,1)S(1)}, bf16[128,1024]{1,0:T(8,128)(2,1)}, u32[]{:S(2)}) copy-start(bf16[128,1024]{1,0:T(8,128)(2,1)} %v_ref.3) | copy-start | bytes 786436
  1.5 3.1 %copy-start.13 = (bf16[128,1024]{1,0:T(8,128)(2,1)S(1)}, bf16[128,1024]{1,0:T(8,128)(2,1)}, u32[]{:S(2)}) copy-start(bf16[128,1024]{1,0:T(8,128)(2,1)} %do_ref.3) | copy-start | bytes 786436
  71.7 1.0 copy-start.14
  72.7 7.8 %copy-start.1 = (bf16[8,128,512]{2,1,0:T(8,128)(2,1)S(1)}, bf16[8,128,512]{2,1,0:T(8,128)(2,1)}, u32[]{:S(2)}) copy-start(bf16[8,128,512]{2,1,0:T(8,128)(2,1)} %get-tuple-element.53.k_ref.v_ref) | copy-start | bytes 3145732
  80.5 2.6 %copy-start.2 = (bf16[8,128,512]{2,1,0:T(8,128)(2,1)S(1)}, bf16[8,128,512]{2,1,0:T(8,128)(2,1)}, u32[]{:S(2)}) copy-start(bf16[8,128,512]{2,1,0:T(8,128)(2,1)} %get-tuple-element.52.qg_ref) | copy-start | bytes 3145732
  80.5 2.6 %copy-start.3 = (f32[4,16,2048]{2,1,0:T(8,128)S(1)}, f32[4,16,2048]{2,1,0:T(8,128)}, u32[]{:S(2)}) copy-start(f32[4,16,2048]{2,1,0:T(8,128)} %get-tuple-element.51.weight_ref) | copy-start | bytes 1572868

commit v3 on v2

--- a/solution.py
+++ b/solution.py
@@ -11,6 +11,7 @@
 AHD = 128
 WINDOW = 1024
 HOP_TICKS = 3
+EARLY = 3
 MESH = pl.DeviceIdType.MESH
 F32 = jnp.float32
 BF16 = jnp.bfloat16
@@ -142,8 +143,8 @@
 def relay_kernel(n, m, span, q_ref, k_ref, v_ref, do_ref, beta_ref, decay_ref, init_ref, next_ref,
                  bw_ref, dw_ref, aq_ref, ak_ref, av_ref, ag_ref,
                  transit_ref, lgrad_ref, t_ref, w_ref, uv_ref, p_ref, n_ref, mem_ref, grad_ref,
-                 weight_ref, kv_ref, qg_ref,
-                 offset_ref, slices, send_f, recv_f, send_b, recv_b, sf_sem, rf_sem, sb_sem, rb_sem,
+                 weight_ref, qg_ref, dquery_ref, stat_ref,
+                 kv_ref, offset_ref, slices, send_f, recv_f, send_b, recv_b, sf_sem, rf_sem, sb_sem, rb_sem,
                  skv_sem, rkv_sem, sqg_sem, rqg_sem, sw_sem, rw_sem):
     me = lax.axis_index("seq")
     head = lax.axis_index("head")
@@ -181,16 +182,20 @@
         peer = lax.rem(head + m - d, m)
         return remote(slices.at[peer], weight_ref.at[peer], sw_sem.at[d], rw_sem.at[d], (me, peer))
 
+    def start_far(d, now):
+        @pl.when(now & (me + d < n))
+        def _():
+            copy_kv(d).start()
+
+        @pl.when(now & (me >= d))
+        def _():
+            copy_qg(d).start()
+
     for d in range(1, m):
         copy_weight(d).start()
     for d in range(1, span):
-        @pl.when(me + d < n)
-        def _(d=d):
-            copy_kv(d).start()
-
-        @pl.when(me >= d)
-        def _(d=d):
-            copy_qg(d).start()
+        if d <= EARLY:
+            start_far(d, True)
 
         @pl.when(me < d)
         def _(d=d):
@@ -202,16 +207,30 @@
 
     lane_count = q_ref.shape[1] // steps
 
-    def local_step(i, carry):
+    def local_step(i):
         lanes = pl.ds(pl.multiple_of(i * lane_count, 128), lane_count)
         mine = pl.ds(i * group, group)
         local_kernel(q_ref.at[:, lanes], k_ref.at[:, lanes], v_ref.at[:, lanes],
                      do_ref.at[:, lanes], beta_ref.at[pl.ds(i, 1)], decay_ref.at[pl.ds(i, 1)],
                      transit_ref.at[mine], offset_ref.at[mine], lgrad_ref.at[mine], t_ref.at[mine],
                      w_ref.at[mine], uv_ref.at[mine], p_ref.at[mine], n_ref.at[mine])
-        return carry
-
-    lax.fori_loop(0, steps, local_step, 0)
+
+    pace = min(HOP_TICKS, group)
+    last_tick = HOP_TICKS * (n - 1) + heads
+    begin_late = HOP_TICKS * jnp.maximum(me, n - 1 - me)
+    apart = begin_late - HOP_TICKS * jnp.minimum(me, n - 1 - me)
+    rows_tick = jnp.where(apart >= heads + 3, begin_late - 4, last_tick)
+
+    def attend():
+        for d in range(1, span):
+            @pl.when(me >= d)
+            def _(d=d):
+                copy_kv(d).wait_recv()
+        for h in range(width // AHD):
+            lanes = slice(h * AHD, (h + 1) * AHD)
+            more = slice(width + h * AHD, width + (h + 1) * AHD)
+            attn_rows(me, aq_ref.at[:, lanes], ag_ref.at[:, lanes], kv_ref.at[:, :, lanes],
+                      kv_ref.at[:, :, more], dquery_ref.at[:, lanes], stat_ref.at[h])
 
     def copy_f(h):
         return pltpu.make_async_remote_copy(
@@ -224,6 +243,17 @@
             recv_sem=rb_sem.at[h], device_id=(left, head), device_id_type=MESH)
 
     def tick(t, carry):
+        @pl.when((t % pace == 0) & (t // pace < steps))
+        def _():
+            local_step(t // pace)
+
+        for d in range(EARLY + 1, span):
+            start_far(d, t == HOP_TICKS * (d - EARLY - 1))
+
+        @pl.when(t == rows_tick)
+        def _():
+            attend()
+
         hf = t - HOP_TICKS * me
         hb = t - HOP_TICKS * (n - 1 - me)
 
@@ -261,7 +291,7 @@
 
         return carry
 
-    lax.fori_loop(0, HOP_TICKS * (n - 1) + heads, tick, 0)
+    lax.fori_loop(0, last_tick + 1, tick, 0)
 
     def drain(h, carry):
         @pl.when(has_right)
@@ -287,7 +317,6 @@
         @pl.when(me >= d)
         def _(d=d):
             copy_qg(d).wait_send()
-            copy_kv(d).wait_recv()
 
 
 def grads_kernel(q_ref, k_ref, v_ref, do_ref, beta_ref, decay_ref, mem_ref, grad_ref,
@@ -340,7 +369,7 @@
         bound_ref[0, j] = mul(transit_ref[j], grad_s, TN) + lgrad_ref[j]
 
 
-def attn_rows_kernel(place_ref, q_ref, g_ref, k_ref, v_ref, dq_ref, stat_ref):
+def attn_rows(place, q_ref, g_ref, k_ref, v_ref, dq_ref, stat_ref):
     size = q_ref.shape[0]
     count = k_ref.shape[0]
     span = count * size
@@ -351,7 +380,7 @@
     cols = lax.broadcasted_iota(jnp.int32, (size, span), 1)
     back = cols // size
     gap = rows - cols % size + back * size
-    allowed = (gap >= 0) & (gap < WINDOW) & (back <= place_ref[0])
+    allowed = (gap >= 0) & (gap < WINDOW) & (back <= place)
     scores = jnp.where(allowed, mul(q_ref[...], keys, NT) * scale, -1e30)
     top = jnp.max(scores, axis=1, keepdims=True)
     weights = jnp.exp(scores - top)
@@ -362,16 +391,16 @@
     dscores = weights * (weight_grad - row_term) * scale
     dq_ref[...] = mul(dscores, keys)
     square = grids(size)
-    stat_ref[0] = jnp.zeros(stat_ref.shape[1:], F32)
-    stat_ref[0, 0:1, :] = as_row(top, *square)
-    stat_ref[0, 1:2, :] = as_row(inverse, *square)
-    stat_ref[0, 2:3, :] = as_row(row_term, *square)
+    stat_ref[...] = jnp.zeros(stat_ref.shape, F32)
+    stat_ref[0:1, :] = as_row(top, *square)
+    stat_ref[1:2, :] = as_row(inverse, *square)
+    stat_ref[2:3, :] = as_row(row_term, *square)
 
 
 def tail_kernel(n, m, span, x_ref, dbeta_ref, ddecay_ref, beta_ref, decay_ref, slope_ref,
                 weight_ref, ak_ref, av_ref, qg_ref, stat_ref,
-                input_ref, wsum_ref, dk_ref, dv_ref,
-                terms, arrived, every, stats, st_sem, rt_sem, se_sem, re_sem, ss_sem, rs_sem):
+                input_ref, wsum_ref, psum_ref, dk_ref, dv_ref,
+                terms, arrived, every, stats, sums, sp_sem, rp_sem, st_sem, rt_sem, se_sem, re_sem, ss_sem, rs_sem):
     me = lax.axis_index("seq")
     head = lax.axis_index("head")
     entered = meet(n, m, me, head)
@@ -383,8 +412,8 @@
     every[head, heads:] = grad_d
     stats[0] = stat_ref[...]
     lane = lax.broadcasted_iota(jnp.int32, (heads, size), 1)
-    params = jnp.where(lane == 0, row_sum(ddecay * decay_ref[...]),
-                       jnp.where(lane == 1, row_sum(grad_d), 0.0))
+    sums[0] = jnp.where(lane == 0, row_sum(ddecay * decay_ref[...]),
+                        jnp.where(lane == 1, row_sum(grad_d), 0.0))
     mine = parts(every[head])
     entered()
 
@@ -400,6 +429,10 @@
         peer = lax.rem(head + m - d, m)
         return remote(every.at[peer], every.at[peer], se_sem.at[d], re_sem.at[d], (me, peer))
 
+    def copy_sum(d):
+        return remote(sums.at[0], sums.at[d], sp_sem.at[d], rp_sem.at[d],
+                      (lax.rem(me + d, n), head))
+
     def copy_term(d):
         return remote(terms.at[d], arrived.at[d], st_sem.at[d], rt_sem.at[d],
                       (lax.rem(me + d, n), head))
@@ -417,13 +450,12 @@
 
     def fill(d):
         place = pl.multiple_of(lax.rem(me + d, n) * part, 128)
-        terms[d] = jnp.zeros(terms.shape[1:], F32)
-        terms[d, :2 * heads] = mul(mine, x_ref[:, pl.ds(place, part)])
-        terms[d, 2 * heads:, :size] = params
+        terms[d] = mul(mine, x_ref[:, pl.ds(place, part)])
 
     def send_term(d, carry):
         fill(d)
         copy_term(d).start()
+        copy_sum(d).start()
         return carry
 
     lax.fori_loop(1, n, send_term, 0)
@@ -459,11 +491,14 @@
     for c in range(0, weight_ref.shape[2], chunk):
         right = weight_ref[:, :, c:c + chunk].reshape(m * 2 * heads, chunk).astype(BF16)
         input_ref[:, c:c + chunk] = mul(left, right, TN)
-    total = terms[0]
+    total, total_sum = terms[0], sums[0]
     for d in range(1, n):
         copy_term(d).wait_recv()
         total = total + arrived[d]
+        copy_sum(d).wait_recv()
+        total_sum = total_sum + sums[d]
     wsum_ref[...] = total
+    psum_ref[...] = total_sum
     for d in range(1, span):
         @pl.when(me >= d)
         def _(d=d):
@@ -472,6 +507,7 @@
         copy_every(d).wait_send()
     for d in range(1, n):
         copy_term(d).wait_send()
+        copy_sum(d).wait_send()
 
 
 def shards(layer_input, beta_weight, decay_weight, log_rate, decay_bias, delta_query, delta_key,
@@ -512,16 +548,16 @@
     beta_steps = betas.reshape(steps, group, size)
     decay_steps = decays.reshape(steps, group, size)
     flops = 2 * heads * size * size * dim
-    (transit, lgrad, inverse, w_all, uv_all, mixing, near, mem_in, grad_end, weight_cols, kv_all,
-     qg_all) = pl.pallas_call(
+    (transit, lgrad, inverse, w_all, uv_all, mixing, near, mem_in, grad_end, weight_cols, qg_all,
+     dquery, stats) = pl.pallas_call(
         functools.partial(relay_kernel, n, m, span),
         out_shape=(state, state, pair, per_token, per_token, pair, pair, state, state,
                    shape(m, 2 * heads, features // m),
                    shape(span, size, 2 * attn_width, kind=BF16),
-                   shape(span, size, 2 * attn_width, kind=BF16)),
+                   shape(size, attn_width), shape(attn_heads, 8, size)),
         in_specs=[vmem] * 14,
-        out_specs=(vmem,) * 12,
-        scratch_shapes=[box, pltpu.VMEM((m, 2 * heads, features // m), F32), box, box, box, box,
+        out_specs=(vmem,) * 13,
+        scratch_shapes=[pltpu.VMEM((span, size, 2 * attn_width), BF16), box, pltpu.VMEM((m, 2 * heads, features // m), F32), box, box, box, box,
                         sem((heads,)), sem((heads,)), sem((heads,)), sem((heads,)),
                         sem((span,)), sem((span,)), sem((span,)), sem((span,)), sem((m,)), sem((m,))],
         compiler_params=params(48, collective_id=0, has_side_effects=True),
@@ -529,22 +565,7 @@
     )(delta_query, delta_key, delta_value, delta_out_grad, beta_steps, decay_steps, state_init,
       state_grad_next, beta_weight, decay_weight, attn_query, attn_key, attn_value, attn_out_grad)
 
-    def own():
-        return pl.BlockSpec((size, AHD), lambda h: (0, h))
-
-    def others(part):
-        return pl.BlockSpec((span, size, AHD), lambda h: (0, 0, part * attn_heads + h))
-
     attn_flops = 2 * size * span * size * attn_width
-    dquery, stats = pl.pallas_call(
-        attn_rows_kernel,
-        grid=(attn_heads,),
-        out_shape=(shape(size, attn_width), shape(attn_heads, 8, size)),
-        in_specs=[pl.BlockSpec(memory_space=pltpu.SMEM), own(), own(), others(0), others(1)],
-        out_specs=(own(), pl.BlockSpec((1, 8, size), lambda h: (h, 0, 0))),
-        compiler_params=params(40), cost_estimate=cost(4 * attn_flops, 3), name="attn_rows",
-    )(me.reshape(1).astype(jnp.int32), attn_query, attn_out_grad, kv_all, kv_all)
-
     tokens = pl.BlockSpec((size, group * dim), lambda i: (0, i))
     gate = pl.BlockSpec((1, group, size), lambda i: (i, 0, 0))
     square = pl.BlockSpec((group, dim, dim), lambda i: (i, 0, 0))
@@ -562,22 +583,23 @@
     )(delta_query, delta_key, delta_value, delta_out_grad, beta_steps, decay_steps,
       mem_in, grad_end, transit, lgrad, inverse, w_all, uv_all, mixing, near)
 
-    slot = pltpu.VMEM((n, 3 * heads, features // n), F32)
-    input_grad, sums, dkey, dvalue = pl.pallas_call(
+    slot = pltpu.VMEM((n, 2 * heads, features // n), F32)
+    input_grad, weights_grad, sums, dkey, dvalue = pl.pallas_call(
         functools.partial(tail_kernel, n, m, span),
-        out_shape=(shape(size, features // m), shape(3 * heads, features // n),
+        out_shape=(shape(size, features // m), shape(2 * heads, features // n), shape(heads, size),
                    shape(size, attn_width), shape(size, attn_width)),
         in_specs=[vmem] * 11,
-        out_specs=(vmem,) * 4,
+        out_specs=(vmem,) * 5,
         scratch_shapes=[slot, slot, pltpu.VMEM((m, 2 * heads, size), F32),
                         pltpu.VMEM((span, attn_heads, 8, size), F32),
+                        pltpu.VMEM((n, heads, size), F32), sem((n,)), sem((n,)),
                         sem((n,)), sem((n,)), sem((m,)), sem((m,)), sem((span,)), sem((span,))],
         compiler_params=params(48, collective_id=1, has_side_effects=True),
         name="tail_exchange", cost_estimate=cost(4 * attn_flops, 6),
     )(layer_input, dbeta.reshape(heads, size), ddecay.reshape(heads, size), betas, decays, slope,
       weight_cols, attn_key, attn_value, qg_all, stats)
-    return (dq, dk, dv, boundary, input_grad, sums[:heads], sums[heads:2 * heads],
-            sums[2 * heads:, 0], sums[2 * heads:, 1], dquery, dkey, dvalue)
+    return (dq, dk, dv, boundary, input_grad, weights_grad[:heads], weights_grad[heads:],
+            sums[:, 0], sums[:, 1], dquery, dkey, dvalue)
 
 
 def solution(mesh):

time: 105 us -> 99.9 us (0.951)
  Pallas kernels: 95.3 us -> 89.6 us
    pallas_call x1, Pallas kernels: 17.9 us -> 14.6 us  [shards(): pl.pallas_call(functools.partial(tail_kernel, n, m, span), out_shape=(sha...]
    pallas_call x1 -> x0, Pallas kernels: 2.6 us -> none  [shards(): pl.pallas_call(attn_rows_kernel, grid=(attn_heads,), out_shape=(shape(siz...]
    dot_general x1, matrix products: 0.64 us -> 2.4 us  [shards(): lax.dot_general(beta_weight, layer_input, NT, preferred_element_type=F32)]
    dot_general x1, matrix products: 2.35 us -> 0.67 us  [shards(): lax.dot_general(decay_weight, layer_input, NT, preferred_element_type=F32)]
    unnamed x33 -> x34, local copies, waits for them, and re-layouts: 3.4 us -> 4.04 us
where the time goes in v3:
time: 99.9 us; the launch traced here: 99.7 us
  Pallas kernels  89.6 us (90%)
  local copies, waits for them, and re-layouts  5.37 us (5%)
  matrix products  3.07 us (3%)
    pallas_call x1, Pallas kernels, shards(): pl.pallas_call(functools.partial(relay_kernel, n, m, span), out_shape=(st...  67.1 us
    pallas_call x1, Pallas kernels, shards(): pl.pallas_call(functools.partial(tail_kernel, n, m, span), out_shape=(sha...  14.6 us
    pallas_call x1, Pallas kernels, shards(): pl.pallas_call(grads_kernel, grid=(steps,), out_shape=(flat, flat, flat,...  7.85 us
    unnamed x34, local copies, waits for them, and re-layouts  4.04 us
    dot_general x1, matrix products, shards(): lax.dot_general(beta_weight, layer_input, NT, preferred_element_type=F32)  2.4 us

profile of v3, /device:TPU:0, one launch (start us, length us, event | category | flops | bytes accessed | tf_op | source)
XLA Modules:
  0.0 99.7 jit_solution(13785344125668068871)
XLA Ops:
  0.6 0.0 copy-start
  0.7 0.0 copy-start.4
  0.7 0.0 copy-start.14
  0.7 0.8 exponential_negate_fusion
  1.5 0.0 copy-start.3
  1.5 0.0 copy-start.5
  1.5 0.0 copy-start.6
  1.5 0.0 copy-start.7
  1.5 0.0 copy-start.8
  1.5 0.0 copy-start.9
  1.5 0.0 copy-start.10
  1.5 0.0 copy-start.11
  1.6 0.0 copy-start.12
  1.6 2.4 %fusion.2.beta_ref = f32[8,128]{1,0:T(8,128)S(1)} fusion(bf16[8,8192]{1,0:T(8,128)(2,1)} %bw_ref.1, bf16[128,8192]{1,0:T(8,128)(2,1)} %x_ref.1), kind=kOutput, calls=%fused_computation.4 | convolution fusion | flops 16780288 | bytes 2232320 | tf_op jit(solution)/shard_map/dot_general | solution.py:528
  4.0 0.0 copy-done
  4.0 0.0 copy-done.4
  4.0 0.0 copy-done.14
  4.0 0.7 divide_multiply_fusion
  4.7 0.0 copy-done.3
  4.7 0.0 copy-done.5
  4.7 0.0 copy-done.6
  4.7 0.0 copy-done.7
  4.7 0.0 copy-done.8
  4.7 0.0 copy-done.9
  4.7 0.0 copy-done.10
  4.8 0.0 copy-done.11
  4.8 0.0 copy-done.12
  4.8 67.1 %state_relay.1 = (f32[8,128,128]{2,1,0:T(8,128)S(1)}, f32[8,128,128]{2,1,0:T(8,128)S(1)}, f32[8,128,128]{2,1,0:T(8,128)S(1)}, f32[8,128,128]{2,1,0:T(8,128)S(1)}...) custom-call(bf16[128,1024]{1,0:T(8,128)(2,1)S(1)} %copy-done.7, ...), custom_call_target="tpu_custom_call" | custom-call | flops 2214592512 | bytes 16777216 | tf_op jit(solution)/shard_map/state_relay/pallas_call | solution.py:552
  71.9 0.0 copy-start.13
  71.9 1.0 %copy-done.13 = f32[8,128,128]{2,1,0:T(8,128)S(1)} copy-done((f32[8,128,128]{2,1,0:T(8,128)S(1)}, f32[8,128,128]{2,1,0:T(8,128)}, u32[]{:S(2)}) %copy-start.13) | copy-done | bytes 524312
  72.9 0.0 copy-start.1
  72.9 0.0 copy-start.2
  72.9 7.8 %delta_grads.1 = (f32[128,1024]{1,0:T(8,128)}, f32[128,1024]{1,0:T(8,128)}, f32[128,1024]{1,0:T(8,128)}, f32[1,8,128,128]{3,2,1,0:T(8,128)}, f32[2,4,128]{2,1,0:T(4,128)S(1)}, /*index=5*/f32[2,4,128]{2,1,0:T(4,128)S(1)}) custom-call(bf16[128,1024]{1,0:T(8,128)(2,1)S(1)} %copy-done.7, bf16[128,1024]{1,0:T(8,128)(2,1)S(1)} %copy-done.8, ...), custom_call_target="tpu_custom_call" | custom-call | flops 1677721600 | bytes 9437184 | tf_op jit(solution)/shard_map/delta_grads/pallas_call | solution.py:575
  80.8 0.0 copy-done.1
  80.8 0.0 copy-done.2
  80.8 14.6 %tail_exchange.1 = (f32[128,2048]{1,0:T(8,128)S(1)}, f32[16,1024]{1,0:T(8,128)S(1)}, f32[8,128]{1,0:T(8,128)S(1)}, f32[128,256]{1,0:T(8,128)S(1)}, f32[128,256]{1,0:T(8,128)S(1)}) custom-call(bf16[128,8192]{1,0:T(8,128)(2,1)S(1)} %copy-done, f32[8,128]{1,0:T(8,128)S(1)} %bitcast.12, f32[8,128]{1,0:T(8,128)S(1)} %bitcast.13, f32[8,128]{1,0:T(8,128)S(1)} %fusion.2.beta_ref, ...), custom_call_target="tpu_custom_call" | custom-call | flops 268435456 | bytes 6291456 | tf_op jit(solution)/shard_map/tail_exchange/pallas_call | solution.py:587
  95.4 0.7 slice_reduce_fusion
  96.1 0.6 fusion.4
  96.7 1.0 copy.31
  97.7 0.7 copy.32
  98.4 0.7 copy.33
  99.0 0.7 copy.34
Async XLA Ops:
  0.6 3.3 %copy-start = (bf16[128,8192]{1,0:T(8,128)(2,1)S(1)}, bf16[128,8192]{1,0:T(8,128)(2,1)}, u32[]{:S(2)}) copy-start(bf16[128,8192]{1,0:T(8,128)(2,1)} %x_ref.1) | copy-start | bytes 6291460
  0.7 3.3 %copy-start.4 = (bf16[8,8192]{1,0:T(8,128)(2,1)S(1)}, bf16[8,8192]{1,0:T(8,128)(2,1)}, u32[]{:S(2)}) copy-start(bf16[8,8192]{1,0:T(8,128)(2,1)} %dw_ref.1) | copy-start | bytes 393220
  0.7 3.3 %copy-start.14 = (f32[8]{0:T(128)S(1)}, f32[8]{0:T(128)}, u32[]{:S(2)}) copy-start(f32[8]{0:T(128)} %param.19) | copy-start | bytes 100
  1.5 3.2 %copy-start.3 = (bf16[8,8192]{1,0:T(8,128)(2,1)S(1)}, bf16[8,8192]{1,0:T(8,128)(2,1)}, u32[]{:S(2)}) copy-start(bf16[8,8192]{1,0:T(8,128)(2,1)} %bw_ref.1) | copy-start | bytes 393220
  1.5 3.2 %copy-start.5 = (bf16[128,256]{1,0:T(8,128)(2,1)S(1)}, bf16[128,256]{1,0:T(8,128)(2,1)}, u32[]{:S(2)}) copy-start(bf16[128,256]{1,0:T(8,128)(2,1)} %ak_ref.3) | copy-start | bytes 196612
  1.5 3.2 %copy-start.6 = (bf16[128,256]{1,0:T(8,128)(2,1)S(1)}, bf16[128,256]{1,0:T(8,128)(2,1)}, u32[]{:S(2)}) copy-start(bf16[128,256]{1,0:T(8,128)(2,1)} %av_ref.3) | copy-start | bytes 196612
  1.5 3.2 %copy-start.7 = (bf16[128,1024]{1,0:T(8,128)(2,1)S(1)}, bf16[128,1024]{1,0:T(8,128)(2,1)}, u32[]{:S(2)}) copy-start(bf16[128,1024]{1,0:T(8,128)(2,1)} %q_ref.3) | copy-start | bytes 786436
  1.5 3.2 %copy-start.8 = (bf16[128,1024]{1,0:T(8,128)(2,1)S(1)}, bf16[128,1024]{1,0:T(8,128)(2,1)}, u32[]{:S(2)}) copy-start(bf16[128,1024]{1,0:T(8,128)(2,1)} %k_ref.3) | copy-start | bytes 786436
  1.5 3.2 %copy-start.9 = (bf16[128,1024]{1,0:T(8,128)(2,1)S(1)}, bf16[128,1024]{1,0:T(8,128)(2,1)}, u32[]{:S(2)}) copy-start(bf16[128,1024]{1,0:T(8,128)(2,1)} %v_ref.3) | copy-start | bytes 786436
  1.5 3.2 %copy-start.10 = (bf16[128,1024]{1,0:T(8,128)(2,1)S(1)}, bf16[128,1024]{1,0:T(8,128)(2,1)}, u32[]{:S(2)}) copy-start(bf16[128,1024]{1,0:T(8,128)(2,1)} %do_ref.3) | copy-start | bytes 786436
  1.5 3.2 %copy-start.11 = (bf16[128,256]{1,0:T(8,128)(2,1)S(1)}, bf16[128,256]{1,0:T(8,128)(2,1)}, u32[]{:S(2)}) copy-start(bf16[128,256]{1,0:T(8,128)(2,1)} %aq_ref.1) | copy-start | bytes 196612
  1.6 3.2 %copy-start.12 = (bf16[128,256]{1,0:T(8,128)(2,1)S(1)}, bf16[128,256]{1,0:T(8,128)(2,1)}, u32[]{:S(2)}) copy-start(bf16[128,256]{1,0:T(8,128)(2,1)} %ag_ref.1) | copy-start | bytes 196612
  71.9 1.0 %copy-start.13 = (f32[8,128,128]{2,1,0:T(8,128)S(1)}, f32[8,128,128]{2,1,0:T(8,128)}, u32[]{:S(2)}) copy-start(f32[8,128,128]{2,1,0:T(8,128)} %get-tuple-element.37.grad_ref) | copy-start | bytes 1572868
  72.9 7.9 %copy-start.1 = (bf16[8,128,512]{2,1,0:T(8,128)(2,1)S(1)}, bf16[8,128,512]{2,1,0:T(8,128)(2,1)}, u32[]{:S(2)}) copy-start(bf16[8,128,512]{2,1,0:T(8,128)(2,1)} %get-tuple-element.52.qg_ref) | copy-start | bytes 3145732
  72.9 7.9 %copy-start.2 = (f32[4,16,2048]{2,1,0:T(8,128)S(1)}, f32[4,16,2048]{2,1,0:T(8,128)}, u32[]{:S(2)}) copy-start(f32[4,16,2048]{2,1,0:T(8,128)} %get-tuple-element.51.weight_ref) | copy-start | bytes 1572868

commit v4 on v3

--- a/solution.py
+++ b/solution.py
@@ -10,7 +10,7 @@
 
 AHD = 128
 WINDOW = 1024
-HOP_TICKS = 3
+HOP_TICKS = 2
 EARLY = 3
 MESH = pl.DeviceIdType.MESH
 F32 = jnp.float32

time: 99.9 us -> 97.4 us (0.975)
  Pallas kernels: 89.6 us -> 87.1 us
    pallas_call x1, Pallas kernels: 14.6 us -> 12.5 us  [shards(): pl.pallas_call(functools.partial(tail_kernel, n, m, span), out_shape=(sha...]
where the time goes in v4:
time: 97.4 us; the launch traced here: 97.2 us
  Pallas kernels  87.1 us (89%)
  local copies, waits for them, and re-layouts  5.37 us (6%)
  matrix products  3.07 us (3%)
    pallas_call x1, Pallas kernels, shards(): pl.pallas_call(functools.partial(relay_kernel, n, m, span), out_shape=(st...  66.7 us
    pallas_call x1, Pallas kernels, shards(): pl.pallas_call(functools.partial(tail_kernel, n, m, span), out_shape=(sha...  12.5 us
    pallas_call x1, Pallas kernels, shards(): pl.pallas_call(grads_kernel, grid=(steps,), out_shape=(flat, flat, flat,...  7.85 us
    unnamed x34, local copies, waits for them, and re-layouts  4.04 us
    dot_general x1, matrix products, shards(): lax.dot_general(beta_weight, layer_input, NT, preferred_element_type=F32)  2.4 us

profile of v4, /device:TPU:0, one launch (start us, length us, event | category | flops | bytes accessed | tf_op | source)
XLA Modules:
  0.0 97.2 jit_solution(5595101092531428853)
XLA Ops:
  0.6 0.0 copy-start
  0.7 0.0 copy-start.4
  0.7 0.0 copy-start.14
  0.7 0.8 exponential_negate_fusion
  1.5 0.0 copy-start.3
  1.5 0.0 copy-start.5
  1.5 0.0 copy-start.6
  1.5 0.0 copy-start.7
  1.5 0.0 copy-start.8
  1.5 0.0 copy-start.9
  1.5 0.0 copy-start.10
  1.5 0.0 copy-start.11
  1.6 0.0 copy-start.12
  1.6 2.4 %fusion.2.beta_ref = f32[8,128]{1,0:T(8,128)S(1)} fusion(bf16[8,8192]{1,0:T(8,128)(2,1)} %bw_ref.1, bf16[128,8192]{1,0:T(8,128)(2,1)} %x_ref.1), kind=kOutput, calls=%fused_computation.4 | convolution fusion | flops 16780288 | bytes 2232320 | tf_op jit(solution)/shard_map/dot_general | solution.py:528
  4.0 0.0 copy-done
  4.0 0.0 copy-done.4
  4.0 0.0 copy-done.14
  4.0 0.7 divide_multiply_fusion
  4.7 0.0 copy-done.3
  4.7 0.0 copy-done.5
  4.7 0.0 copy-done.6
  4.7 0.0 copy-done.7
  4.7 0.0 copy-done.8
  4.7 0.0 copy-done.9
  4.7 0.0 copy-done.10
  4.8 0.0 copy-done.11
  4.8 0.0 copy-done.12
  4.8 66.7 %state_relay.1 = (f32[8,128,128]{2,1,0:T(8,128)S(1)}, f32[8,128,128]{2,1,0:T(8,128)S(1)}, f32[8,128,128]{2,1,0:T(8,128)S(1)}, f32[8,128,128]{2,1,0:T(8,128)S(1)}...) custom-call(bf16[128,1024]{1,0:T(8,128)(2,1)S(1)} %copy-done.7, ...), custom_call_target="tpu_custom_call" | custom-call | flops 2214592512 | bytes 16777216 | tf_op jit(solution)/shard_map/state_relay/pallas_call | solution.py:552
  71.5 0.0 copy-start.13
  71.5 1.0 %copy-done.13 = f32[8,128,128]{2,1,0:T(8,128)S(1)} copy-done((f32[8,128,128]{2,1,0:T(8,128)S(1)}, f32[8,128,128]{2,1,0:T(8,128)}, u32[]{:S(2)}) %copy-start.13) | copy-done | bytes 524312
  72.6 0.0 copy-start.1
  72.6 0.0 copy-start.2
  72.6 7.9 %delta_grads.1 = (f32[128,1024]{1,0:T(8,128)}, f32[128,1024]{1,0:T(8,128)}, f32[128,1024]{1,0:T(8,128)}, f32[1,8,128,128]{3,2,1,0:T(8,128)}, f32[2,4,128]{2,1,0:T(4,128)S(1)}, /*index=5*/f32[2,4,128]{2,1,0:T(4,128)S(1)}) custom-call(bf16[128,1024]{1,0:T(8,128)(2,1)S(1)} %copy-done.7, bf16[128,1024]{1,0:T(8,128)(2,1)S(1)} %copy-done.8, ...), custom_call_target="tpu_custom_call" | custom-call | flops 1677721600 | bytes 9437184 | tf_op jit(solution)/shard_map/delta_grads/pallas_call | solution.py:575
  80.4 0.0 copy-done.1
  80.4 0.0 copy-done.2
  80.4 12.5 %tail_exchange.1 = (f32[128,2048]{1,0:T(8,128)S(1)}, f32[16,1024]{1,0:T(8,128)S(1)}, f32[8,128]{1,0:T(8,128)S(1)}, f32[128,256]{1,0:T(8,128)S(1)}, f32[128,256]{1,0:T(8,128)S(1)}) custom-call(bf16[128,8192]{1,0:T(8,128)(2,1)S(1)} %copy-done, f32[8,128]{1,0:T(8,128)S(1)} %bitcast.12, f32[8,128]{1,0:T(8,128)S(1)} %bitcast.13, f32[8,128]{1,0:T(8,128)S(1)} %fusion.2.beta_ref, ...), custom_call_target="tpu_custom_call" | custom-call | flops 268435456 | bytes 6291456 | tf_op jit(solution)/shard_map/tail_exchange/pallas_call | solution.py:587
  92.9 0.7 slice_reduce_fusion
  93.6 0.6 fusion.4
  94.2 1.0 copy.31
  95.2 0.7 copy.32
  95.9 0.7 copy.33
  96.5 0.7 copy.34
Async XLA Ops:
  0.6 3.3 %copy-start = (bf16[128,8192]{1,0:T(8,128)(2,1)S(1)}, bf16[128,8192]{1,0:T(8,128)(2,1)}, u32[]{:S(2)}) copy-start(bf16[128,8192]{1,0:T(8,128)(2,1)} %x_ref.1) | copy-start | bytes 6291460
  0.7 3.3 %copy-start.4 = (bf16[8,8192]{1,0:T(8,128)(2,1)S(1)}, bf16[8,8192]{1,0:T(8,128)(2,1)}, u32[]{:S(2)}) copy-start(bf16[8,8192]{1,0:T(8,128)(2,1)} %dw_ref.1) | copy-start | bytes 393220
  0.7 3.3 %copy-start.14 = (f32[8]{0:T(128)S(1)}, f32[8]{0:T(128)}, u32[]{:S(2)}) copy-start(f32[8]{0:T(128)} %param.19) | copy-start | bytes 100
  1.5 3.2 %copy-start.3 = (bf16[8,8192]{1,0:T(8,128)(2,1)S(1)}, bf16[8,8192]{1,0:T(8,128)(2,1)}, u32[]{:S(2)}) copy-start(bf16[8,8192]{1,0:T(8,128)(2,1)} %bw_ref.1) | copy-start | bytes 393220
  1.5 3.2 %copy-start.5 = (bf16[128,256]{1,0:T(8,128)(2,1)S(1)}, bf16[128,256]{1,0:T(8,128)(2,1)}, u32[]{:S(2)}) copy-start(bf16[128,256]{1,0:T(8,128)(2,1)} %ak_ref.3) | copy-start | bytes 196612
  1.5 3.2 %copy-start.6 = (bf16[128,256]{1,0:T(8,128)(2,1)S(1)}, bf16[128,256]{1,0:T(8,128)(2,1)}, u32[]{:S(2)}) copy-start(bf16[128,256]{1,0:T(8,128)(2,1)} %av_ref.3) | copy-start | bytes 196612
  1.5 3.2 %copy-start.7 = (bf16[128,1024]{1,0:T(8,128)(2,1)S(1)}, bf16[128,1024]{1,0:T(8,128)(2,1)}, u32[]{:S(2)}) copy-start(bf16[128,1024]{1,0:T(8,128)(2,1)} %q_ref.3) | copy-start | bytes 786436
  1.5 3.2 %copy-start.8 = (bf16[128,1024]{1,0:T(8,128)(2,1)S(1)}, bf16[128,1024]{1,0:T(8,128)(2,1)}, u32[]{:S(2)}) copy-start(bf16[128,1024]{1,0:T(8,128)(2,1)} %k_ref.3) | copy-start | bytes 786436
  1.5 3.2 %copy-start.9 = (bf16[128,1024]{1,0:T(8,128)(2,1)S(1)}, bf16[128,1024]{1,0:T(8,128)(2,1)}, u32[]{:S(2)}) copy-start(bf16[128,1024]{1,0:T(8,128)(2,1)} %v_ref.3) | copy-start | bytes 786436
  1.5 3.2 %copy-start.10 = (bf16[128,1024]{1,0:T(8,128)(2,1)S(1)}, bf16[128,1024]{1,0:T(8,128)(2,1)}, u32[]{:S(2)}) copy-start(bf16[128,1024]{1,0:T(8,128)(2,1)} %do_ref.3) | copy-start | bytes 786436
  1.5 3.2 %copy-start.11 = (bf16[128,256]{1,0:T(8,128)(2,1)S(1)}, bf16[128,256]{1,0:T(8,128)(2,1)}, u32[]{:S(2)}) copy-start(bf16[128,256]{1,0:T(8,128)(2,1)} %aq_ref.1) | copy-start | bytes 196612
  1.6 3.2 %copy-start.12 = (bf16[128,256]{1,0:T(8,128)(2,1)S(1)}, bf16[128,256]{1,0:T(8,128)(2,1)}, u32[]{:S(2)}) copy-start(bf16[128,256]{1,0:T(8,128)(2,1)} %ag_ref.1) | copy-start | bytes 196612
  71.5 1.0 %copy-start.13 = (f32[8,128,128]{2,1,0:T(8,128)S(1)}, f32[8,128,128]{2,1,0:T(8,128)}, u32[]{:S(2)}) copy-start(f32[8,128,128]{2,1,0:T(8,128)} %get-tuple-element.37.grad_ref) | copy-start | bytes 1572868
  72.6 7.9 %copy-start.1 = (bf16[8,128,512]{2,1,0:T(8,128)(2,1)S(1)}, bf16[8,128,512]{2,1,0:T(8,128)(2,1)}, u32[]{:S(2)}) copy-start(bf16[8,128,512]{2,1,0:T(8,128)(2,1)} %get-tuple-element.52.qg_ref) | copy-start | bytes 3145732
  72.6 7.9 %copy-start.2 = (f32[4,16,2048]{2,1,0:T(8,128)S(1)}, f32[4,16,2048]{2,1,0:T(8,128)}, u32[]{:S(2)}) copy-start(f32[4,16,2048]{2,1,0:T(8,128)} %get-tuple-element.51.weight_ref) | copy-start | bytes 1572868
